TPU v7x, 256 devices: a whole 4x4x8 slice. The times are simulated.
256 devices in a mesh: rows: 64 (over y, z, core), cell: 4 (over x).
Axes of the slice: x: 4, y: 4, z: 8, core: 2. Of those that a mesh axis runs over, the one named last changes fastest.
Arguments:
- covariates: bfloat16 [1048576, 128], P('rows'), may hold values from -6 to 6, as said below
- outcomes: float32 [8, 1048576], P(None, 'rows'), may hold values from -60 to 60
- multipliers: bfloat16 [1048576, 512], P('rows', 'cell'), may hold values from -5 to 5
- cohorts: int32 [8192], P('rows'), may hold values from 3 to 8, as said below
- cells: int32 [4, 2], P('cell'), may hold values from 3 to 7, as said below
Outputs:
- influence: float32 [4, 1048576], P('cell', 'rows')
- bootstrap: float32 [4, 512], P(None, 'cell')
Inputs may be any that keep to these rules, and one draw needn't show every extreme that they name: `cohorts`: blocks are in non-decreasing order of cohort, and every cohort from 3 to 8 holds at least one block. `cells`: each cell's period is at least its group. `covariates`: column 0 is 1 for every worker.
All inputs are finite; a program needn't handle non-finite values.
Results may differ from a plain program's by a relative error of at most 0.006.
The roundings to bfloat16 on the way count: a program that leaves them out, or rounds other values in their place, can miss the bound.
Values may be sent and summed in bfloat16 or wider, within the bound.
No kernel may reach another device: no remote copies, remote signals or barrier semaphores. Data moves between devices by JAX's collectives and lax.ppermute only.
A program may use at most 128 MiB of HBM per device.

v0:
```python
import functools
import math

import jax
import jax.numpy as jnp
from jax import lax
from jax.experimental import pallas as pl
from jax.experimental.pallas import tpu as pltpu
from jax.sharding import Mesh, PartitionSpec as P

ROWS = ("y", "z", "core")
F32 = jnp.float32
BF16 = jnp.bfloat16
WIDTH = 128
HALF = 64
CHUNK = 2048
PACKED = 40
VMEM = pl.BlockSpec(memory_space=pltpu.VMEM)
SMEM = pl.BlockSpec(memory_space=pltpu.SMEM)
HBM = pl.BlockSpec(memory_space=pltpu.HBM)
FREE = pl.BlockSpec()
PARAMS = pltpu.CompilerParams(vmem_limit_bytes=24 << 20)


def shape(*dims, dtype=F32):
    return jax.ShapeDtypeStruct(dims, dtype)


def iota(dims, axis):
    return lax.broadcasted_iota(jnp.int32, dims, axis)


def fold(gram):
    top, low = gram[:HALF], gram[HALF:]
    row, col = iota((HALF, WIDTH), 0), iota((HALF, WIDTH), 1)
    folded = jnp.where((col < HALF) & (col > row), pltpu.roll(low, HALF, 1), top)
    diagonal = jnp.sum(jnp.where(col - HALF == row, low, 0.0), axis=0, keepdims=True)
    return folded, diagonal


def unfold(folded, diagonal):
    row, col = iota((HALF, WIDTH), 0), iota((HALF, WIDTH), 1)
    turned = jnp.concatenate([folded, jnp.zeros_like(folded)], axis=0).T
    top = jnp.where((col >= HALF) | (col <= row), folded, turned[:HALF])
    right = col - HALF
    low = jnp.where(
        right > row,
        pltpu.roll(folded, HALF, 1),
        jnp.where(right < row, pltpu.roll(turned[:HALF], HALF, 1), diagonal),
    )
    return top, jnp.where(col < HALF, turned[HALF:], low)


def write_payload(out, folded, extras):
    pad = jnp.zeros((7, WIDTH), F32)
    for p in range(out.shape[0]):
        h = p % 2
        out[p, 0:32, :] = folded[32 * h : 32 * h + 32]
        out[p, 32:40, :] = jnp.concatenate([extras[h], pad], axis=0)


def summed(ref):
    total = ref[0]
    for p in range(1, ref.shape[0]):
        total = total + ref[p]
    return total


def lane(block, i):
    return jnp.broadcast_to(block[:, i : i + 1], block.shape)


def sub(block, i):
    return jnp.broadcast_to(block[i : i + 1, :], block.shape)


def scaled_panel(panel, k):
    row, col = iota((8, WIDTH), 0), iota((8, WIDTH), 1) - 8 * k
    inside = (col >= 0) & (col < 8)
    columns = [lane(panel, 8 * k + j) for j in range(8)]
    out = jnp.where(inside, jnp.where(col == row, 1.0, 0.0), panel)
    for j in range(8):
        inverse = 1.0 / sub(columns[j], j)
        here = row == j
        factor = jnp.where(here, 0.0, columns[j])

        def step(block):
            pivot = sub(block, j) * inverse
            return jnp.where(here, pivot, block) - factor * pivot

        out = step(out)
        for m in range(j + 1, 8):
            columns[m] = step(columns[m])
    return out, inside


def swept(blocks):
    count = len(blocks)
    for k in range(count):
        scaled, inside = scaled_panel(blocks[k], k)
        new = []
        for i in range(count):
            if i == k:
                new.append(jnp.where(inside, -scaled, scaled))
                continue
            change = lane(blocks[i], 8 * k) * sub(scaled, 0)
            for j in range(1, 8):
                change = change + lane(blocks[i], 8 * k + j) * sub(scaled, j)
            new.append(jnp.where(inside, change, blocks[i] - change))
        blocks = new
    return blocks


def solve(top, low, vector):
    blocks = [top[8 * i : 8 * i + 8] for i in range(8)] + [low[8 * i : 8 * i + 8] for i in range(8)]
    inverse = jnp.concatenate(swept(blocks), axis=0)
    return -jnp.dot(
        jnp.broadcast_to(vector, (8, WIDTH)),
        inverse,
        precision=lax.Precision.HIGHEST,
        preferred_element_type=F32,
    )


def halves(core, own, other):
    is_first = core == 0
    first = jnp.where(is_first, own, other)
    second = jnp.where(is_first, other, own)
    folded = jnp.concatenate([first[:32], second[:32]], axis=0)
    return folded, first[32:33], second[32:33]


def arrivals(source, target, sems, axis):
    copies = []
    for i in range(target.shape[axis] // CHUNK):
        span = pl.ds(i * CHUNK, CHUNK)
        place = (span, slice(None)) if axis == 0 else (slice(None), span)
        copies.append(pltpu.make_async_copy(source.at[place], target.at[place], sems.at[i]))
        copies[-1].start()
    return copies


def chunk_of(i):
    return slice(i * CHUNK, (i + 1) * CHUNK)


def flag(condition, dtype=F32):
    return jnp.where(condition, 1.0, 0.0).astype(dtype)


def first_kernel(
    cells_hbm, cohorts_hbm, x_hbm, y_hbm, x, xt, xt_hbm, out, cells, cohorts, y, x_sems, y_sems, xt_sems, sems
):
    per = CHUNK // WIDTH
    small = [
        pltpu.make_async_copy(cells_hbm, cells, sems.at[0]),
        pltpu.make_async_copy(cohorts_hbm, cohorts, sems.at[1]),
    ]
    for copy in small:
        copy.start()
    x_copies = arrivals(x_hbm, x, x_sems, 0)
    y_copies = arrivals(y_hbm, y, y_sems, 1)
    for copy in small:
        copy.wait()
    group, period = cells[0, 0], cells[0, 1]
    total = jnp.zeros((WIDTH + 16, WIDTH), F32)
    changes = jnp.zeros((1, WIDTH), F32)
    sent = []
    for i, copy in enumerate(x_copies):
        copy.wait()
        here = x[chunk_of(i), :]
        turned = here.T
        xt[:, chunk_of(i)] = turned
        span = pl.ds(i * CHUNK, CHUNK)
        sent.append(pltpu.make_async_copy(xt.at[:, span], xt_hbm.at[:, span], xt_sems.at[i]))
        sent[-1].start()
        left, marks = [], []
        for b in range(per):
            cohort = cohorts[i * per + b]
            treated = flag(cohort == group)
            eligible = treated + flag(cohort > period)
            left.append(turned[:, b * WIDTH : (b + 1) * WIDTH] * eligible.astype(BF16))
            marks.append(jnp.full((16, WIDTH), treated, F32).astype(BF16))
        left = jnp.concatenate([jnp.concatenate(left, axis=1), jnp.concatenate(marks, axis=1)], axis=0)
        total = total + jnp.dot(left, here, preferred_element_type=F32)
    for copy in y_copies:
        copy.wait()
    change = y[pl.ds(period, 1), :] - y[pl.ds(group - 1, 1), :]
    for b in range(cohorts.shape[0]):
        changes = changes + flag(cohorts[b] == group) * change[:, b * WIDTH : (b + 1) * WIDTH]
    folded, diagonal = fold(total[:WIDTH])
    scalar = jnp.sum(changes, axis=1, keepdims=True)
    first_lane = iota((1, WIDTH), 1) == 0
    write_payload(out, folded, (total[WIDTH : WIDTH + 1], jnp.where(first_lane, scalar, diagonal)))
    for copy in sent:
        copy.wait()


def control_kernel(cells, cohorts, x, xt, y, out):
    group, period = cells[0, 0], cells[0, 1]
    per = CHUNK // WIDTH
    total = jnp.zeros((WIDTH + 16, WIDTH), F32)
    for i in range(x.shape[0] // CHUNK):
        span = pl.ds(i * CHUNK, CHUNK)
        change = y[pl.ds(period, 1), span] - y[pl.ds(group - 1, 1), span]
        change = jnp.broadcast_to(change, (16, CHUNK)).astype(BF16)
        turned = jnp.concatenate([xt[:, chunk_of(i)], change], axis=0)
        left = []
        for b in range(per):
            control = flag(cohorts[i * per + b] > period).astype(BF16)
            left.append(turned[:, b * WIDTH : (b + 1) * WIDTH] * control)
        left = jnp.concatenate(left, axis=1)
        total = total + jnp.dot(left, x[chunk_of(i), :], preferred_element_type=F32)
    folded, diagonal = fold(total[:WIDTH])
    out[0:64, :] = folded
    out[64:72, :] = jnp.concatenate(
        [total[WIDTH : WIDTH + 1], diagonal, jnp.zeros((6, WIDTH), F32)], axis=0
    )


def newton_kernel(
    first, cells, cohorts, own, other, x, xt, before, control, coefs, keep, out
):
    group, period = cells[0, 0], cells[0, 1]
    per = CHUNK // WIDTH
    mine = summed(own)
    folded, row, diagonal = halves(lax.axis_index("core"), mine[:40], summed(other)[:40])
    top, low = unfold(folded, diagonal)
    if first:
        keep[...] = jnp.concatenate([row, diagonal, jnp.zeros((6, WIDTH), F32)], axis=0)
        new = 4.0 * solve(top, low, row - 0.5 * top[0:1])
    else:
        keep[...] = mine[32:40]
        new = before[...] + solve(top, low, row)
    coefs[...] = new
    rounded = jnp.concatenate([new, new], axis=0).astype(BF16)
    total = jnp.zeros((WIDTH + 16, WIDTH), F32)
    for i in range(x.shape[0] // CHUNK):
        turned = xt[:, chunk_of(i)]
        index = jnp.dot(rounded, turned, preferred_element_type=F32)
        probability = jax.nn.sigmoid(index)
        weight = probability * (1.0 - probability)
        left, errors = [], []
        for b in range(per):
            cohort = cohorts[i * per + b]
            treated = flag(cohort == group)
            eligible = treated + flag(cohort > period)
            span = slice(b * WIDTH, (b + 1) * WIDTH)
            here = jnp.broadcast_to(weight[0:1, span] * eligible, (WIDTH, WIDTH))
            left.append((here * turned[:, span].astype(F32)).astype(BF16))
            errors.append(((treated - probability[:, span]) * eligible).astype(BF16))
        left = jnp.concatenate([jnp.concatenate(left, axis=1), jnp.concatenate(errors, axis=1)], axis=0)
        total = total + jnp.dot(left, x[chunk_of(i), :], preferred_element_type=F32)
    folded, diagonal = fold(total[:WIDTH])
    write_payload(out, folded, (total[WIDTH : WIDTH + 1], diagonal))
    for p in range(out.shape[0]):
        if first:
            out[p, 33:35, :] = control[64:66, :]
            out[p, 40:48, :] = control[8 * p : 8 * p + 8, :]
        else:
            out[p, 40:48, :] = mine[40:48]


def control_solve_kernel(arrived, extras, y_hbm, mult_hbm, out, y, mult, y_sems, mult_sems):
    copies = arrivals(mult_hbm, mult, mult_sems, 0) + arrivals(y_hbm, y, y_sems, 1)
    folded = jnp.concatenate([arrived[p, 40:48, :] for p in range(arrived.shape[0])], axis=0)
    solved = solve(*unfold(folded, extras[2:3, :]), extras[1:2, :])
    out[...] = solved.astype(BF16).astype(F32)
    for copy in copies:
        copy.wait()


def last_kernel(cells, own, other, control, before, keep, xt_hbm, out, xt, xt_sems):
    copies = arrivals(xt_hbm, xt, xt_sems, 1)
    folded, row, diagonal = halves(lax.axis_index("core"), summed(own), summed(other))
    new = before[...] + solve(*unfold(folded, diagonal), row)
    ols = control[0:1, :]
    treated_x = keep[0:1, :]
    count = lane(treated_x, 0)
    fitted = jnp.sum(ols * treated_x, axis=1, keepdims=True)
    mean = (lane(keep[1:2, :], 0) - fitted) / count
    out[...] = jnp.concatenate(
        [
            new[0:1].astype(BF16).astype(F32),
            ols,
            mean,
            count,
            jnp.full((1, WIDTH), cells[0, 0].astype(F32), F32),
            jnp.full((1, WIDTH), cells[0, 1].astype(F32), F32),
            jnp.zeros((2, WIDTH), F32),
        ],
        axis=0,
    )
    for copy in copies:
        copy.wait()


def draws_kernel(
    cohorts, m0, m1, m2, m3, xt, y, mult, out, treated_out, product_out, odds_out
):
    per = CHUNK // WIDTH
    blank = jnp.zeros((4, WIDTH), F32)

    def stacked(i):
        return jnp.concatenate([m[i : i + 1, :] for m in (m0, m1, m2, m3)] + [blank], axis=0)

    left = jnp.concatenate([stacked(0), stacked(1)], axis=0).astype(BF16)
    mean, count, group, period = stacked(2), stacked(3), stacked(4), stacked(5)
    valid = iota((8, WIDTH), 0) < 4
    per_count = jnp.where(valid, 1.0 / jnp.where(valid, count, 1.0), 0.0)
    group = jnp.where(valid, group, -1.0)
    period = jnp.where(valid, period, 99.0)
    signs = [flag(period == p) - flag(group - 1.0 == p) for p in range(8)]
    total = jnp.zeros((48, WIDTH), F32)
    odds_sum = jnp.zeros((8, WIDTH), F32)
    product_sum = jnp.zeros((8, WIDTH), F32)
    for i in range(xt.shape[1] // CHUNK):
        both = jnp.dot(left, xt[:, chunk_of(i)], preferred_element_type=F32)
        parts = []
        for b in range(per):
            span = slice(b * WIDTH, (b + 1) * WIDTH)
            place = slice(i * CHUNK + b * WIDTH, i * CHUNK + (b + 1) * WIDTH)
            cohort = cohorts[i * per + b].astype(F32)
            outcome = y[:, place]
            change = signs[0] * sub(outcome, 0)
            for p in range(1, 8):
                change = change + signs[p] * sub(outcome, p)
            residual = change - both[8:16, span]
            treated = jnp.where(group == cohort, (residual - mean) * per_count, 0.0)
            odds = jnp.where(period < cohort, jnp.exp(both[0:8, span]), 0.0)
            product = odds * residual
            odds_sum = odds_sum + odds
            product_sum = product_sum + product
            treated_out[:, place] = treated[0:1]
            product_out[:, place] = product[0:1]
            odds_out[:, place] = odds[0:1]
            pairs = []
            for value in (treated, product, odds):
                high = value.astype(BF16).astype(F32)
                pairs.append(jnp.concatenate([high, value - high], axis=0).astype(BF16))
            parts.append(jnp.concatenate(pairs, axis=0))
        total = total + jnp.dot(
            jnp.concatenate(parts, axis=1), mult[chunk_of(i), :], preferred_element_type=F32
        )
    col = iota((8, WIDTH), 1)
    both = jnp.where(
        col == 0,
        jnp.sum(odds_sum, axis=1, keepdims=True),
        jnp.where(col == 1, jnp.sum(product_sum, axis=1, keepdims=True), 0.0),
    )
    rows = [(total[16 * s : 16 * s + 8] + total[16 * s + 8 : 16 * s + 16])[0:4] for s in range(3)]
    rows = jnp.concatenate(rows + [both[0:4]], axis=0)
    for p in range(out.shape[0]):
        out[p] = rows


def relay_kernel(arrived, out):
    rows = out.shape[1]
    total = summed(arrived)[:rows]
    for p in range(out.shape[0]):
        out[p] = total


def finish_kernel(total_rows, arrived, treated, product, odds, influence, bootstrap):
    cell = lax.axis_index("cell")
    sums = summed(arrived)
    weight = lane(sums[12:16], 0)
    mean = lane(sums[12:16], 1) / weight
    draws = math.sqrt(total_rows) * (sums[0:4] - (sums[4:8] - mean * sums[8:12]) / weight)
    for slot in range(4):
        bootstrap[pl.ds(cell ^ slot, 1), :] = draws[slot : slot + 1]
    scale = total_rows / weight[0:1, 0:1]
    influence[...] = total_rows * treated[...] - scale * (product[...] - mean[0:1, 0:1] * odds[...])


def swap_cores(value):
    return lax.ppermute(value, "core", [(0, 1), (1, 0)])


def to_pairs(payload):
    return lax.all_to_all(payload, ("y", "core"), 0, 0)


def to_line(arrived, rows):
    peers = lax.axis_size("z")
    copies = call(relay_kernel, "relay", [shape(peers, rows, WIDTH)], [VMEM])(arrived)
    return lax.all_to_all(copies[0], "z", 0, 0)


def call(kernel, name, outs, ins, out_specs=None, scratch=(), cost=None):
    return pl.pallas_call(
        kernel,
        out_shape=outs,
        in_specs=ins,
        out_specs=out_specs or [VMEM] * len(outs),
        scratch_shapes=list(scratch),
        compiler_params=PARAMS,
        cost_estimate=cost,
        name=name,
    )


def shards(covariates, outcomes, multipliers, cohorts, cells):
    rows_here = covariates.shape[0]
    total_rows = rows_here * lax.axis_size(ROWS)
    pairs = lax.axis_size(("y", "core"))
    sems = pltpu.SemaphoreType.DMA((rows_here // CHUNK,))
    vector = shape(1, rows_here)
    eight = shape(8, WIDTH)
    cost = pl.CostEstimate(flops=1 << 33, bytes_accessed=10 << 20, transcendentals=0)
    tall, wide, wide_hbm, payload = call(
        first_kernel,
        "first",
        [
            shape(rows_here, WIDTH, dtype=BF16),
            shape(WIDTH, rows_here, dtype=BF16),
            pltpu.HBM((WIDTH, rows_here), BF16),
            shape(pairs, 40, WIDTH),
        ],
        [HBM] * 4,
        [FREE, FREE, HBM, VMEM],
        [
            pltpu.SMEM(cells.shape, jnp.int32),
            pltpu.SMEM(cohorts.shape, jnp.int32),
            pltpu.VMEM(outcomes.shape, F32),
            sems,
            sems,
            sems,
            pltpu.SemaphoreType.DMA((2,)),
        ],
    )(*(pltpu.with_memory_space_constraint(v, pltpu.HBM) for v in (cells, cohorts, covariates, outcomes)))
    halfway = to_pairs(payload)
    arrived = to_line(halfway, 40)
    control = call(
        control_kernel, "control", [shape(72, WIDTH)], [SMEM, SMEM, FREE, FREE, FREE], cost=cost
    )(cells, cohorts, tall, wide, outcomes)[0]
    coefs = jnp.zeros((8, WIDTH), F32)
    kept = []
    for step in range(2):
        coefs, keep, payload = call(
            functools.partial(newton_kernel, step == 0),
            "newton",
            [eight, eight, shape(pairs, 48, WIDTH)],
            [SMEM, SMEM, VMEM, VMEM, FREE, FREE, VMEM, VMEM],
        )(cells, cohorts, arrived, swap_cores(arrived), tall, wide, coefs, control)
        kept.append(keep)
        halfway = to_pairs(payload)
        arrived = to_line(halfway, 48 if step == 0 else 40)
    far = [pltpu.with_memory_space_constraint(v, pltpu.HBM) for v in (outcomes, multipliers, wide_hbm)]
    ols, deep, mult = call(
        control_solve_kernel,
        "ols",
        [eight, shape(*outcomes.shape), shape(rows_here, WIDTH, dtype=BF16)],
        [VMEM, VMEM, HBM, HBM],
        [VMEM, FREE, FREE],
        [sems, sems],
        cost,
    )(halfway, kept[1], *far[:2])
    arrived, ols = lax.optimization_barrier((arrived, ols))
    message, wide = call(
        last_kernel,
        "last",
        [eight, shape(WIDTH, rows_here, dtype=BF16)],
        [SMEM] + [VMEM] * 5 + [HBM],
        [VMEM, FREE],
        [sems],
    )(cells, arrived, swap_cores(arrived), ols, coefs, kept[0], far[2])
    messages = [message] + [
        lax.ppermute(message, "cell", [(i, i ^ s) for i in range(4)]) for s in range(1, 4)
    ]
    payload, treated, product, odds = call(
        draws_kernel,
        "draws",
        [shape(pairs, 16, WIDTH), vector, vector, vector],
        [SMEM] + [VMEM] * 4 + [FREE] * 3,
    )(cohorts, *messages, wide, deep, mult)
    arrived = to_line(to_pairs(payload), 16)
    return call(
        functools.partial(finish_kernel, total_rows),
        "finish",
        [vector, shape(4, WIDTH)],
        [VMEM] * 4,
    )(arrived, treated, product, odds)


def solution(mesh):
    fine = Mesh(mesh.devices.reshape(4, 8, 2, 4), ROWS + ("cell",))
    return jax.shard_map(
        shards,
        mesh=fine,
        in_specs=(P(ROWS, None), P(None, ROWS), P(ROWS, "cell"), P(ROWS), P("cell", None)),
        out_specs=(P("cell", ROWS), P(None, "cell")),
        check_vma=False,
    )
```

profile of v0, /device:TPU:1, one launch (start us, length us, event | category | flops | bytes accessed | tf_op | source)
XLA Modules:
  0.0 140.6 jit_solution(14746125389047872886)
XLA Ops:
  0.6 0.0 copy-start.2
  0.7 5.0 %first.1 = (bf16[16384,128]{1,0:T(8,128)(2,1)S(1)}, bf16[128,16384]{1,0:T(8,128)(2,1)S(1)}, bf16[128,16384]{1,0:T(8,128)(2,1)}, f32[8,40,128]{2,1,0:T(8,128)S(1)}) custom-call(s32[1,2]{1,0:T(1,128)} %cells.7, s32[128]{0:T(128)} %cohorts.7, bf16[16384,128]{1,0:T(8,128)(2,1)} %x_hbm.1, f32[8,16384]{1,0:T(8,128)} %y_hbm.3), custom_call_target="tpu_custom_call" | custom-call | tf_op jit(solution)/shard_map/first/pallas_call | solution.py:411
  5.7 11.4 %all_to_all.40.arrived = f32[8,40,128]{2,1,0:T(8,128)S(1)} all-to-all(f32[8,40,128]{2,1,0:T(8,128)S(1)} %get-tuple-element.23), channel_id=1, replica_groups=mesh['y'=4,'z'=8,'core'=2,'cell'=4] {'y','core'}, dimensions={0} | all-to-all | bytes 327680 | tf_op jit(solution)/shard_map/all_to_all | solution.py:381
  17.0 16.0 %all_to_all.41.own = f32[8,40,128]{2,1,0:T(8,128)S(1)} all-to-all(f32[8,40,128]{2,1,0:T(8,128)S(1)} %relay.4), channel_id=1, replica_groups=mesh['y'=4,'z'=8,'core'=2,'cell'=4] {'z'}, dimensions={0} | all-to-all | bytes 327680 | tf_op jit(solution)/shard_map/all_to_all | solution.py:387
  33.1 2.7 %collective-permute-start = (f32[8,40,128]{2,1,0:T(8,128)S(1)}, f32[8,40,128]{2,1,0:T(8,128)S(1)}, u32[]{:S(2)}, u32[]{:S(2)}) collective-permute-start(f32[8,40,128]{2,1,0:T(8,128)S(1)} %all_to_all.41.own), channel_id=1, source_target_pairs={{0,4},{4,0},{1,5},{5,1},{2,6},{6,2},{3,7},{7,3},{8,12},{12,8},{9,1... | collective-permute-start | bytes 491528 | tf_op jit(solution)/shard_map/ppermute | solution.py:377
  35.7 2.0 %control.1 = f32[72,128]{1,0:T(8,128)S(1)} custom-call(s32[1,2]{1,0:T(1,128)S(1)} %copy-done.4, s32[128]{0:T(128)S(1)} %copy-done.3, bf16[16384,128]{1,0:T(8,128)(2,1)S(1)} %get-tuple-element.24.x, bf16[128,16384]{1,0:T(8,128)(2,1)S(1)} %get-tuple-element.25.xt, f32[8,16384]{1,0:T(8,128)S(1)} %copy-done.2), custom_call_target="tpu_custom_call" | custom-call | flops 8589934592 | bytes 10485760 | tf_op jit(solution)/shard_map/control/pallas_call | solution.py:434
  37.7 0.0 collective-permute-done.other
  37.8 8.6 %newton.2 = (f32[8,128]{1,0:T(8,128)S(1)}, f32[8,128]{1,0:T(8,128)S(1)}, f32[8,48,128]{2,1,0:T(8,128)S(1)}) custom-call(s32[1,2]{1,0:T(1,128)S(1)} %copy-done.4, s32[128]{0:T(128)S(1)} %copy-done.3, f32[8,40,128]{2,1,0:T(8,128)S(1)} %all_to_all.41.own, f32[8,40,128]{2,1,0:T(8,128)S(1)} %collective-permute-done.other, ...), custom_call_target="tpu_custom_call" | custom-call | tf_op jit(solution)/shard_map/newton/pallas_call | solution.py:440
  46.3 8.3 %all_to_all.42.arrived = f32[8,48,128]{2,1,0:T(8,128)S(1)} all-to-all(f32[8,48,128]{2,1,0:T(8,128)S(1)} %get-tuple-element.26), channel_id=1, replica_groups=mesh['y'=4,'z'=8,'core'=2,'cell'=4] {'y','core'}, dimensions={0} | all-to-all | bytes 393216 | tf_op jit(solution)/shard_map/all_to_all | solution.py:381
  54.7 11.0 %all_to_all.43.own = f32[8,48,128]{2,1,0:T(8,128)S(1)} all-to-all(f32[8,48,128]{2,1,0:T(8,128)S(1)} %relay.5), channel_id=1, replica_groups=mesh['y'=4,'z'=8,'core'=2,'cell'=4] {'z'}, dimensions={0} | all-to-all | bytes 393216 | tf_op jit(solution)/shard_map/all_to_all | solution.py:387
  65.7 2.8 %collective-permute-start.1 = (f32[8,48,128]{2,1,0:T(8,128)S(1)}, f32[8,48,128]{2,1,0:T(8,128)S(1)}, u32[]{:S(2)}, u32[]{:S(2)}) collective-permute-start(f32[8,48,128]{2,1,0:T(8,128)S(1)} %all_to_all.43.own), channel_id=1, source_target_pairs={{0,4},{4,0},{1,5},{5,1},{2,6},{6,2},{3,7},{7,3},{8,12},{12,8},{9,1... | collective-permute-start | bytes 589832 | tf_op jit(solution)/shard_map/ppermute | solution.py:377
  68.5 1.1 collective-permute-done.1.other
  69.6 8.6 %newton.3 = (f32[8,128]{1,0:T(8,128)S(1)}, f32[8,128]{1,0:T(8,128)S(1)}, f32[8,48,128]{2,1,0:T(8,128)S(1)}) custom-call(s32[1,2]{1,0:T(1,128)S(1)} %copy-done.4, s32[128]{0:T(128)S(1)} %copy-done.3, f32[8,48,128]{2,1,0:T(8,128)S(1)} %all_to_all.43.own, f32[8,48,128]{2,1,0:T(8,128)S(1)} %collective-permute-done.1.other, ...), custom_call_target="tpu_custom_call" | custom-call | tf_op jit(solution)/shard_map/newton/pallas_call | solution.py:440
  78.1 8.7 %all_to_all.44.arrived = f32[8,48,128]{2,1,0:T(8,128)S(1)} all-to-all(f32[8,48,128]{2,1,0:T(8,128)S(1)} %get-tuple-element.28), channel_id=1, replica_groups=mesh['y'=4,'z'=8,'core'=2,'cell'=4] {'y','core'}, dimensions={0} | all-to-all | bytes 393216 | tf_op jit(solution)/shard_map/all_to_all | solution.py:381
  86.8 0.7 relay.6
  87.5 3.4 %all-to-all-start.5 = ((f32[8,40,128]{2,1,0:T(8,128)}), f32[8,40,128]{2,1,0:T(8,128)S(1)}, u32[]{:S(2)}, u32[]{:S(2)}) async-start(f32[8,40,128]{2,1,0:T(8,128)} %relay.6), calls=%async_computation.5 | async-start | bytes 327680 | tf_op jit(solution)/shard_map/all_to_all | solution.py:387
  90.9 6.3 %ols.1 = (f32[8,128]{1,0:T(8,128)S(1)}, f32[8,16384]{1,0:T(8,128)S(1)}, bf16[16384,128]{1,0:T(8,128)(2,1)S(1)}) custom-call(f32[8,48,128]{2,1,0:T(8,128)S(1)} %all_to_all.44.arrived, f32[8,128]{1,0:T(8,128)S(1)} %get-tuple-element.29.extras, f32[8,16384]{1,0:T(8,128)} %y_hbm.3, bf16[16384,128]{1,0:T(8,128)(2,1)} %mult_hbm.1), custom_call_target="tpu_custom_call" | custom-call | flops 8589934592 | bytes 10485760 | tf_op jit(solution)/shard_map/ols/pallas_call | solution.py:450
  97.2 2.0 %copy-done = bf16[16384,128]{1,0:T(8,128)(2,1)} copy-done((bf16[16384,128]{1,0:T(8,128)(2,1)}, bf16[16384,128]{1,0:T(8,128)(2,1)S(1)}, u32[]{:S(2)}) %copy-start) | copy-done | bytes 4194328
  99.2 0.0 all-to-all-done.5.own
  99.2 2.3 %collective-permute-start.2 = (f32[8,40,128]{2,1,0:T(8,128)S(1)}, f32[8,40,128]{2,1,0:T(8,128)S(1)}, u32[]{:S(2)}, u32[]{:S(2)}) collective-permute-start(f32[8,40,128]{2,1,0:T(8,128)S(1)} %all-to-all-done.5.own), channel_id=1, source_target_pairs={{0,4},{4,0},{1,5},{5,1},{2,6},{6,2},{3,7},{7,3},{8,12},{12,8},{9,1... | collective-permute-start | bytes 491528 | tf_op jit(solution)/shard_map/ppermute | solution.py:377
  101.5 1.0 collective-permute-done.2.other
  102.5 6.7 %last.1 = (f32[8,128]{1,0:T(8,128)S(1)}, bf16[128,16384]{1,0:T(8,128)(2,1)S(1)}) custom-call(s32[1,2]{1,0:T(1,128)S(1)} %copy-done.4, f32[8,40,128]{2,1,0:T(8,128)S(1)} %all-to-all-done.5.own, f32[8,40,128]{2,1,0:T(8,128)S(1)} %collective-permute-done.2.other, f32[8,128]{1,0:T(8,128)S(1)} %get-tuple-element.32.control, ...), custom_call_target="tpu_custom_call" | custom-call | tf_op jit(solution)/shard_map/last/pallas_call | solution.py:460
  109.3 2.6 %collective-permute-start.5 = (f32[8,128]{1,0:T(8,128)S(1)}, f32[8,128]{1,0:T(8,128)S(1)}, u32[]{:S(2)}, u32[]{:S(2)}) collective-permute-start(f32[8,128]{1,0:T(8,128)S(1)} %get-tuple-element.36.m0), channel_id=1, source_target_pairs={{0,3},{1,2},{2,1},{3,0},{4,7},{5,6},{6,5},{7,4},{8,11},{9,10},{10,... | collective-permute-start | bytes 12296 | tf_op jit(solution)/shard_map/ppermute | solution.py:469
  111.8 0.5 collective-permute-start.4
  112.4 0.3 collective-permute-start.3
  112.6 0.4 collective-permute-done.5.m3
  113.0 2.8 %collective-permute-done.4.m2 = f32[8,128]{1,0:T(8,128)S(1)} collective-permute-done((f32[8,128]{1,0:T(8,128)S(1)}, f32[8,128]{1,0:T(8,128)S(1)}, u32[]{:S(2)}, u32[]{:S(2)}) %collective-permute-start.4) | collective-permute-done | bytes 4128 | tf_op jit(solution)/shard_map/ppermute | solution.py:469
  115.8 0.0 collective-permute-done.3.m1
  115.8 2.4 %draws.1 = (f32[8,16,128]{2,1,0:T(8,128)S(1)}, f32[1,16384]{1,0:T(1,128)S(1)}, f32[1,16384]{1,0:T(1,128)S(1)}, f32[1,16384]{1,0:T(1,128)S(1)}) custom-call(s32[128]{0:T(128)S(1)} %copy-done.3, f32[8,128]{1,0:T(8,128)S(1)} %get-tuple-element.36.m0, f32[8,128]{1,0:T(8,128)S(1)} %collective-permute-done.3.m1, f32[8,128]{1,0:T(8,128)S(1)} %collective-permute-done.4.m2, ...), custom_call_target="tpu_custom_call" | custom-call | tf_op jit(solution)/shard_map/draws/pallas_call | solution.py:471
  118.2 9.0 %all_to_all.45.arrived = f32[8,16,128]{2,1,0:T(8,128)S(1)} all-to-all(f32[8,16,128]{2,1,0:T(8,128)S(1)} %get-tuple-element.40), channel_id=1, replica_groups=mesh['y'=4,'z'=8,'core'=2,'cell'=4] {'y','core'}, dimensions={0} | all-to-all | bytes 131072 | tf_op jit(solution)/shard_map/all_to_all | solution.py:381
  127.2 12.5 %all_to_all.46.arrived = f32[8,16,128]{2,1,0:T(8,128)S(1)} all-to-all(f32[8,16,128]{2,1,0:T(8,128)S(1)} %relay.7), channel_id=1, replica_groups=mesh['y'=4,'z'=8,'core'=2,'cell'=4] {'z'}, dimensions={0} | all-to-all | bytes 131072 | tf_op jit(solution)/shard_map/all_to_all | solution.py:387
  139.8 0.8 finish.1
  (12 shorter events, 0.1 us)
Async XLA Ops:
  0.6 35.1 %copy-start.4 = (s32[1,2]{1,0:T(1,128)S(1)}, s32[1,2]{1,0:T(1,128)}, u32[]{:S(2)}) copy-start(s32[1,2]{1,0:T(1,128)} %cells.7) | copy-start | bytes 28
  0.6 35.1 %copy-start.3 = (s32[128]{0:T(128)S(1)}, s32[128]{0:T(128)}, u32[]{:S(2)}) copy-start(s32[128]{0:T(128)} %cohorts.7) | copy-start | bytes 1540
  0.6 35.1 %copy-start.2 = (f32[8,16384]{1,0:T(8,128)S(1)}, f32[8,16384]{1,0:T(8,128)}, u32[]{:S(2)}) copy-start(f32[8,16384]{1,0:T(8,128)} %y_hbm.3) | copy-start | bytes 1572868
  33.1 4.7 %collective-permute-start = (f32[8,40,128]{2,1,0:T(8,128)S(1)}, f32[8,40,128]{2,1,0:T(8,128)S(1)}, u32[]{:S(2)}, u32[]{:S(2)}) collective-permute-start(f32[8,40,128]{2,1,0:T(8,128)S(1)} %all_to_all.41.own), channel_id=1, source_target_pairs={{0,4},{4,0},{1,5},{5,1},{2,6},{6,2},{3,7},{7,3},{8,12},{12,8},{9,1... | collective-permute-start | bytes 491528 | tf_op jit(solution)/shard_map/ppermute | solution.py:377
  65.7 3.9 %collective-permute-start.1 = (f32[8,48,128]{2,1,0:T(8,128)S(1)}, f32[8,48,128]{2,1,0:T(8,128)S(1)}, u32[]{:S(2)}, u32[]{:S(2)}) collective-permute-start(f32[8,48,128]{2,1,0:T(8,128)S(1)} %all_to_all.43.own), channel_id=1, source_target_pairs={{0,4},{4,0},{1,5},{5,1},{2,6},{6,2},{3,7},{7,3},{8,12},{12,8},{9,1... | collective-permute-start | bytes 589832 | tf_op jit(solution)/shard_map/ppermute | solution.py:377
  87.5 11.7 %all-to-all-start.5 = ((f32[8,40,128]{2,1,0:T(8,128)}), f32[8,40,128]{2,1,0:T(8,128)S(1)}, u32[]{:S(2)}, u32[]{:S(2)}) async-start(f32[8,40,128]{2,1,0:T(8,128)} %relay.6), calls=%async_computation.5 | async-start | bytes 327680 | tf_op jit(solution)/shard_map/all_to_all | solution.py:387
  97.2 2.0 %copy-start = (bf16[16384,128]{1,0:T(8,128)(2,1)}, bf16[16384,128]{1,0:T(8,128)(2,1)S(1)}, u32[]{:S(2)}) copy-start(bf16[16384,128]{1,0:T(8,128)(2,1)S(1)} %get-tuple-element.39.mult) | copy-start | bytes 12582916
  99.2 16.6 %copy-start.1 = (bf16[16384,128]{1,0:T(8,128)(2,1)S(1)}, bf16[16384,128]{1,0:T(8,128)(2,1)}, u32[]{:S(2)}) copy-start(bf16[16384,128]{1,0:T(8,128)(2,1)} %copy-done) | copy-start | bytes 12582916
  99.2 3.3 %collective-permute-start.2 = (f32[8,40,128]{2,1,0:T(8,128)S(1)}, f32[8,40,128]{2,1,0:T(8,128)S(1)}, u32[]{:S(2)}, u32[]{:S(2)}) collective-permute-start(f32[8,40,128]{2,1,0:T(8,128)S(1)} %all-to-all-done.5.own), channel_id=1, source_target_pairs={{0,4},{4,0},{1,5},{5,1},{2,6},{6,2},{3,7},{7,3},{8,12},{12,8},{9,1... | collective-permute-start | bytes 491528 | tf_op jit(solution)/shard_map/ppermute | solution.py:377
  109.3 3.8 %collective-permute-start.5 = (f32[8,128]{1,0:T(8,128)S(1)}, f32[8,128]{1,0:T(8,128)S(1)}, u32[]{:S(2)}, u32[]{:S(2)}) collective-permute-start(f32[8,128]{1,0:T(8,128)S(1)} %get-tuple-element.36.m0), channel_id=1, source_target_pairs={{0,3},{1,2},{2,1},{3,0},{4,7},{5,6},{6,5},{7,4},{8,11},{9,10},{10,... | collective-permute-start | bytes 12296 | tf_op jit(solution)/shard_map/ppermute | solution.py:469
  111.8 4.0 %collective-permute-start.4 = (f32[8,128]{1,0:T(8,128)S(1)}, f32[8,128]{1,0:T(8,128)S(1)}, u32[]{:S(2)}, u32[]{:S(2)}) collective-permute-start(f32[8,128]{1,0:T(8,128)S(1)} %get-tuple-element.36.m0), channel_id=1, source_target_pairs={{0,2},{1,3},{2,0},{3,1},{4,6},{5,7},{6,4},{7,5},{8,10},{9,11},{10,... | collective-permute-start | bytes 12296 | tf_op jit(solution)/shard_map/ppermute | solution.py:469
  112.4 3.4 %collective-permute-start.3 = (f32[8,128]{1,0:T(8,128)S(1)}, f32[8,128]{1,0:T(8,128)S(1)}, u32[]{:S(2)}, u32[]{:S(2)}) collective-permute-start(f32[8,128]{1,0:T(8,128)S(1)} %get-tuple-element.36.m0), channel_id=1, source_target_pairs={{0,1},{1,0},{2,3},{3,2},{4,5},{5,4},{6,7},{7,6},{8,9},{9,8},{10,11... | collective-permute-start | bytes 12296 | tf_op jit(solution)/shard_map/ppermute | solution.py:469
where the time goes:
time: 141 us
  blocking collectives  76.9 us (55%)
  Pallas kernels  41.2 us (29%)
  starting transfers between devices  14.5 us (10%)
  waiting for transfers between devices  5.29 us (4%)
  local copies, waits for them, and re-layouts  2 us (1%)
    all_to_all x3, blocking collectives, to_line(): return lax.all_to_all(copies[0], 'z', 0, 0)  39.6 us
    all_to_all x4, blocking collectives, to_pairs(): return lax.all_to_all(payload, ('y', 'core'), 0, 0)  37.3 us
    pallas_call x2, Pallas kernels, shards(): call(functools.partial(newton_kernel, step == 0), 'newton', [eight, eight...  17.2 us
    ppermute x3, starting transfers between devices, swap_cores(): return lax.ppermute(value, 'core', [(0, 1), (1, 0)])  7.75 us
    pallas_call x1, Pallas kernels, shards(): call(last_kernel, 'last', [eight, shape(WIDTH, rows_here, dtype=BF16)], [...  6.74 us
    pallas_call x1, Pallas kernels, shards(): call(control_solve_kernel, 'ols', [eight, shape(*outcomes.shape), shape(r...  6.35 us
    pallas_call x1, Pallas kernels, shards(): call(first_kernel, 'first', [shape(rows_here, WIDTH, dtype=BF16), shape(W...  4.98 us
    all_to_all x1, starting transfers between devices, to_line(): return lax.all_to_all(copies[0], 'z', 0, 0)  3.38 us
  transfers between devices with their start and end apart: 7, of which 4 were waited for; matrix products, arithmetic and copies ran while one was open for 0% of the time, Pallas kernels for 6%

commit v1 on v0

--- a/solution.py
+++ b/solution.py
@@ -13,7 +13,7 @@
 BF16 = jnp.bfloat16
 WIDTH = 128
 HALF = 64
-CHUNK = 2048
+CHUNK = 4096
 PACKED = 40
 VMEM = pl.BlockSpec(memory_space=pltpu.VMEM)
 SMEM = pl.BlockSpec(memory_space=pltpu.SMEM)
@@ -74,52 +74,53 @@
     return jnp.broadcast_to(block[i : i + 1, :], block.shape)
 
 
-def scaled_panel(panel, k):
-    row, col = iota((8, WIDTH), 0), iota((8, WIDTH), 1) - 8 * k
-    inside = (col >= 0) & (col < 8)
-    columns = [lane(panel, 8 * k + j) for j in range(8)]
-    out = jnp.where(inside, jnp.where(col == row, 1.0, 0.0), panel)
-    for j in range(8):
-        inverse = 1.0 / sub(columns[j], j)
-        here = row == j
-        factor = jnp.where(here, 0.0, columns[j])
-
-        def step(block):
-            pivot = sub(block, j) * inverse
-            return jnp.where(here, pivot, block) - factor * pivot
-
-        out = step(out)
-        for m in range(j + 1, 8):
-            columns[m] = step(columns[m])
-    return out, inside
-
-
-def swept(blocks):
-    count = len(blocks)
-    for k in range(count):
-        scaled, inside = scaled_panel(blocks[k], k)
-        new = []
-        for i in range(count):
-            if i == k:
-                new.append(jnp.where(inside, -scaled, scaled))
-                continue
-            change = lane(blocks[i], 8 * k) * sub(scaled, 0)
-            for j in range(1, 8):
-                change = change + lane(blocks[i], 8 * k + j) * sub(scaled, j)
-            new.append(jnp.where(inside, change, blocks[i] - change))
-        blocks = new
-    return blocks
+def tree(terms):
+    while len(terms) > 1:
+        terms = [terms[i] + terms[i + 1] for i in range(0, len(terms), 2)]
+    return terms[0]
 
 
 def solve(top, low, vector):
     blocks = [top[8 * i : 8 * i + 8] for i in range(8)] + [low[8 * i : 8 * i + 8] for i in range(8)]
-    inverse = jnp.concatenate(swept(blocks), axis=0)
-    return -jnp.dot(
-        jnp.broadcast_to(vector, (8, WIDTH)),
-        inverse,
-        precision=lax.Precision.HIGHEST,
-        preferred_element_type=F32,
-    )
+    blocks.append(jnp.broadcast_to(vector, (8, WIDTH)))
+    row = iota((8, WIDTH), 0)
+    columns = [lane(blocks[0], m) for m in range(8)]
+    for k in range(16):
+        col = iota((8, WIDTH), 1) - 8 * k
+        inside = (col >= 0) & (col < 8)
+        scaled = jnp.where(inside, jnp.where(col == row, 1.0, 0.0), blocks[k])
+        ahead = [lane(blocks[k], 8 * k + 8 + m) for m in range(8)] if k < 15 else []
+        for j in range(0, 8, 2):
+            left, right = columns[j], columns[j + 1]
+            a, b, d = sub(left, j), sub(right, j), sub(right, j + 1)
+            scale = 1.0 / (a * d - b * b)
+            a, b, d = a * scale, b * scale, d * scale
+            here, there = row == j, row == j + 1
+            pair = here | there
+            first = jnp.where(here, -d, jnp.where(there, b, left * d - right * b))
+            second = jnp.where(here, b, jnp.where(there, -a, right * a - left * b))
+
+            def step(block):
+                return jnp.where(pair, 0.0, block) - first * sub(block, j) - second * sub(block, j + 1)
+
+            for m in range(j + 2, 8):
+                columns[m] = step(columns[m])
+            ahead = [step(block) for block in ahead]
+            scaled = step(scaled)
+        if k < 15:
+            factors = [lane(blocks[k + 1], 8 * k + j) for j in range(8)]
+            columns = [
+                lane(blocks[k + 1], 8 * k + 8 + m)
+                - tree([factors[j] * sub(ahead[m], j) for j in range(8)])
+                for m in range(8)
+            ]
+        rows = [sub(scaled, j) for j in range(8)]
+        for i in range(k + 1, 17):
+            change = lane(blocks[i], 8 * k) * rows[0]
+            for j in range(1, 8):
+                change = change + lane(blocks[i], 8 * k + j) * rows[j]
+            blocks[i] = jnp.where(inside, change, blocks[i] - change)
+    return blocks[16]
 
 
 def halves(core, own, other):
@@ -237,7 +238,7 @@
     total = jnp.zeros((WIDTH + 16, WIDTH), F32)
     for i in range(x.shape[0] // CHUNK):
         turned = xt[:, chunk_of(i)]
-        index = jnp.dot(rounded, turned, preferred_element_type=F32)
+        index = jnp.dot(rounded, turned, preferred_element_type=F32)[0:8]
         probability = jax.nn.sigmoid(index)
         weight = probability * (1.0 - probability)
         left, errors = [], []
@@ -248,7 +249,8 @@
             span = slice(b * WIDTH, (b + 1) * WIDTH)
             here = jnp.broadcast_to(weight[0:1, span] * eligible, (WIDTH, WIDTH))
             left.append((here * turned[:, span].astype(F32)).astype(BF16))
-            errors.append(((treated - probability[:, span]) * eligible).astype(BF16))
+            error = (treated - probability[:, span]) * eligible
+            errors.append(jnp.concatenate([error, error], axis=0).astype(BF16))
         left = jnp.concatenate([jnp.concatenate(left, axis=1), jnp.concatenate(errors, axis=1)], axis=0)
         total = total + jnp.dot(left, x[chunk_of(i), :], preferred_element_type=F32)
     folded, diagonal = fold(total[:WIDTH])
@@ -261,17 +263,13 @@
             out[p, 40:48, :] = mine[40:48]
 
 
-def control_solve_kernel(arrived, extras, y_hbm, mult_hbm, out, y, mult, y_sems, mult_sems):
-    copies = arrivals(mult_hbm, mult, mult_sems, 0) + arrivals(y_hbm, y, y_sems, 1)
+def control_solve_kernel(arrived, extras, out):
     folded = jnp.concatenate([arrived[p, 40:48, :] for p in range(arrived.shape[0])], axis=0)
     solved = solve(*unfold(folded, extras[2:3, :]), extras[1:2, :])
     out[...] = solved.astype(BF16).astype(F32)
-    for copy in copies:
-        copy.wait()
-
-
-def last_kernel(cells, own, other, control, before, keep, xt_hbm, out, xt, xt_sems):
-    copies = arrivals(xt_hbm, xt, xt_sems, 1)
+
+
+def last_kernel(cells, own, other, control, before, keep, out):
     folded, row, diagonal = halves(lax.axis_index("core"), summed(own), summed(other))
     new = before[...] + solve(*unfold(folded, diagonal), row)
     ols = control[0:1, :]
@@ -291,7 +289,11 @@
         ],
         axis=0,
     )
-    for copy in copies:
+
+
+def bring_kernel(message, xt_hbm, y_hbm, mult_hbm, xt, y, mult, xt_sems, y_sems, mult_sems):
+    copies = arrivals(xt_hbm, xt, xt_sems, 1) + arrivals(y_hbm, y, y_sems, 1)
+    for copy in copies + arrivals(mult_hbm, mult, mult_sems, 0):
         copy.wait()
 
 
@@ -446,25 +448,23 @@
         kept.append(keep)
         halfway = to_pairs(payload)
         arrived = to_line(halfway, 48 if step == 0 else 40)
-    far = [pltpu.with_memory_space_constraint(v, pltpu.HBM) for v in (outcomes, multipliers, wide_hbm)]
-    ols, deep, mult = call(
-        control_solve_kernel,
-        "ols",
-        [eight, shape(*outcomes.shape), shape(rows_here, WIDTH, dtype=BF16)],
-        [VMEM, VMEM, HBM, HBM],
-        [VMEM, FREE, FREE],
-        [sems, sems],
+    ols = call(control_solve_kernel, "ols", [eight], [VMEM, VMEM], cost=cost)(halfway, kept[1])[0]
+    arrived, ols = lax.optimization_barrier((arrived, ols))
+    message = call(last_kernel, "last", [eight], [SMEM] + [VMEM] * 5)(
+        cells, arrived, swap_cores(arrived), ols, coefs, kept[0]
+    )[0]
+    wide, deep, mult = call(
+        bring_kernel,
+        "bring",
+        [shape(WIDTH, rows_here, dtype=BF16), shape(*outcomes.shape), shape(rows_here, WIDTH, dtype=BF16)],
+        [VMEM] + [HBM] * 3,
+        [FREE] * 3,
+        [sems, sems, sems],
         cost,
-    )(halfway, kept[1], *far[:2])
-    arrived, ols = lax.optimization_barrier((arrived, ols))
-    message, wide = call(
-        last_kernel,
-        "last",
-        [eight, shape(WIDTH, rows_here, dtype=BF16)],
-        [SMEM] + [VMEM] * 5 + [HBM],
-        [VMEM, FREE],
-        [sems],
-    )(cells, arrived, swap_cores(arrived), ols, coefs, kept[0], far[2])
+    )(
+        message,
+        *(pltpu.with_memory_space_constraint(v, pltpu.HBM) for v in (wide_hbm, outcomes, multipliers)),
+    )
     messages = [message] + [
         lax.ppermute(message, "cell", [(i, i ^ s) for i in range(4)]) for s in range(1, 4)
     ]

time: 141 us -> 131 us (0.929)
  Pallas kernels: 41.2 us -> 34.9 us
  blocking collectives: 76.9 us -> 73.6 us
  local copies, waits for them, and re-layouts: 2 us -> 0.02 us
  waiting for transfers between devices: 5.29 us -> 6.72 us
    all_to_all x1, waiting for transfers between devices: 0.01 us -> 4.61 us  [to_line(): return lax.all_to_all(copies[0], 'z', 0, 0)]
    pallas_call x2, Pallas kernels: 17.2 us -> 13.6 us  [shards(): call(functools.partial(newton_kernel, step == 0), 'newton', [eight, eight...]
    ppermute x3, waiting for transfers between devices: 3.19 us -> 0.01 us  [shards(): lax.ppermute(message, 'cell', [(i, i ^ s) for i in range(4)])]
    all_to_all x3, blocking collectives: 39.6 us -> 36.7 us  [to_line(): return lax.all_to_all(copies[0], 'z', 0, 0)]
    unnamed x10 -> x6, local copies, waits for them, and re-layouts: 2 us -> 0.01 us
    pallas_call x2 -> x3, Pallas kernels: 13.1 us -> 11.1 us  [the longest x1 4.01 us: shards(): call(last_kernel, 'last', [eight], [SMEM] + [VMEM] * 5)]
  transfers between devices with their start and end apart: 7 -> 7, of which waited for: 4 -> 3; matrix products, arithmetic and copies ran while one was open for 0% -> 0% of each run, Pallas kernels for 6% -> 7%
where the time goes in v1:
time: 131 us
  blocking collectives  73.6 us (56%)
  Pallas kernels  34.9 us (27%)
  starting transfers between devices  14.8 us (11%)
  waiting for transfers between devices  6.72 us (5%)
    all_to_all x4, blocking collectives, to_pairs(): return lax.all_to_all(payload, ('y', 'core'), 0, 0)  36.8 us
    all_to_all x3, blocking collectives, to_line(): return lax.all_to_all(copies[0], 'z', 0, 0)  36.7 us
    pallas_call x2, Pallas kernels, shards(): call(functools.partial(newton_kernel, step == 0), 'newton', [eight, eight...  13.6 us
    ppermute x3, starting transfers between devices, swap_cores(): return lax.ppermute(value, 'core', [(0, 1), (1, 0)])  8.04 us
    all_to_all x1, waiting for transfers between devices, to_line(): return lax.all_to_all(copies[0], 'z', 0, 0)  4.61 us
    pallas_call x1, Pallas kernels, shards(): call(first_kernel, 'first', [shape(rows_here, WIDTH, dtype=BF16), shape(W...  4.51 us
    pallas_call x1, Pallas kernels, shards(): call(last_kernel, 'last', [eight], [SMEM] + [VMEM] * 5)  4.01 us
    pallas_call x1, Pallas kernels, shards(): call(bring_kernel, 'bring', [shape(WIDTH, rows_here, dtype=BF16), shape(*...  3.66 us
  transfers between devices with their start and end apart: 7, of which 3 were waited for; matrix products, arithmetic and copies ran while one was open for 0% of the time, Pallas kernels for 7%

profile of v1, /device:TPU:1, one launch (start us, length us, event | category | flops | bytes accessed | tf_op | source)
XLA Modules:
  0.0 130.7 jit_solution(2901637140852177965)
XLA Ops:
  0.6 0.0 copy-start
  0.7 4.5 %first.1 = (bf16[16384,128]{1,0:T(8,128)(2,1)S(1)}, bf16[128,16384]{1,0:T(8,128)(2,1)S(1)}, bf16[128,16384]{1,0:T(8,128)(2,1)}, f32[8,40,128]{2,1,0:T(8,128)S(1)}) custom-call(s32[1,2]{1,0:T(1,128)} %cells.7, s32[128]{0:T(128)} %cohorts.7, bf16[16384,128]{1,0:T(8,128)(2,1)} %x_hbm.1, f32[8,16384]{1,0:T(8,128)} %y_hbm.3), custom_call_target="tpu_custom_call" | custom-call | tf_op jit(solution)/shard_map/first/pallas_call | solution.py:413
  5.2 11.4 %all_to_all.40.arrived = f32[8,40,128]{2,1,0:T(8,128)S(1)} all-to-all(f32[8,40,128]{2,1,0:T(8,128)S(1)} %get-tuple-element.21), channel_id=1, replica_groups=mesh['y'=4,'z'=8,'core'=2,'cell'=4] {'y','core'}, dimensions={0} | all-to-all | bytes 327680 | tf_op jit(solution)/shard_map/all_to_all | solution.py:383
  16.6 16.0 %all_to_all.41.own = f32[8,40,128]{2,1,0:T(8,128)S(1)} all-to-all(f32[8,40,128]{2,1,0:T(8,128)S(1)} %relay.4), channel_id=1, replica_groups=mesh['y'=4,'z'=8,'core'=2,'cell'=4] {'z'}, dimensions={0} | all-to-all | bytes 327680 | tf_op jit(solution)/shard_map/all_to_all | solution.py:389
  32.6 2.7 %collective-permute-start = (f32[8,40,128]{2,1,0:T(8,128)S(1)}, f32[8,40,128]{2,1,0:T(8,128)S(1)}, u32[]{:S(2)}, u32[]{:S(2)}) collective-permute-start(f32[8,40,128]{2,1,0:T(8,128)S(1)} %all_to_all.41.own), channel_id=1, source_target_pairs={{0,4},{4,0},{1,5},{5,1},{2,6},{6,2},{3,7},{7,3},{8,12},{12,8},{9,1... | collective-permute-start | bytes 491528 | tf_op jit(solution)/shard_map/ppermute | solution.py:379
  35.3 2.0 %control.1 = f32[72,128]{1,0:T(8,128)S(1)} custom-call(s32[1,2]{1,0:T(1,128)S(1)} %copy-done.1, s32[128]{0:T(128)S(1)} %copy-done.2, bf16[16384,128]{1,0:T(8,128)(2,1)S(1)} %get-tuple-element.22.x, bf16[128,16384]{1,0:T(8,128)(2,1)S(1)} %get-tuple-element.23.xt, f32[8,16384]{1,0:T(8,128)S(1)} %copy-done), custom_call_target="tpu_custom_call" | custom-call | flops 8589934592 | bytes 10485760 | tf_op jit(solution)/shard_map/control/pallas_call | solution.py:436
  37.3 0.0 collective-permute-done.other
  37.3 6.8 %newton.2 = (f32[8,128]{1,0:T(8,128)S(1)}, f32[8,128]{1,0:T(8,128)S(1)}, f32[8,48,128]{2,1,0:T(8,128)S(1)}) custom-call(s32[1,2]{1,0:T(1,128)S(1)} %copy-done.1, s32[128]{0:T(128)S(1)} %copy-done.2, f32[8,40,128]{2,1,0:T(8,128)S(1)} %all_to_all.41.own, f32[8,40,128]{2,1,0:T(8,128)S(1)} %collective-permute-done.other, ...), custom_call_target="tpu_custom_call" | custom-call | tf_op jit(solution)/shard_map/newton/pallas_call | solution.py:442
  44.1 8.3 %all_to_all.42.arrived = f32[8,48,128]{2,1,0:T(8,128)S(1)} all-to-all(f32[8,48,128]{2,1,0:T(8,128)S(1)} %get-tuple-element.24), channel_id=1, replica_groups=mesh['y'=4,'z'=8,'core'=2,'cell'=4] {'y','core'}, dimensions={0} | all-to-all | bytes 393216 | tf_op jit(solution)/shard_map/all_to_all | solution.py:383
  52.4 11.0 %all_to_all.43.own = f32[8,48,128]{2,1,0:T(8,128)S(1)} all-to-all(f32[8,48,128]{2,1,0:T(8,128)S(1)} %relay.5), channel_id=1, replica_groups=mesh['y'=4,'z'=8,'core'=2,'cell'=4] {'z'}, dimensions={0} | all-to-all | bytes 393216 | tf_op jit(solution)/shard_map/all_to_all | solution.py:389
  63.5 2.8 %collective-permute-start.1 = (f32[8,48,128]{2,1,0:T(8,128)S(1)}, f32[8,48,128]{2,1,0:T(8,128)S(1)}, u32[]{:S(2)}, u32[]{:S(2)}) collective-permute-start(f32[8,48,128]{2,1,0:T(8,128)S(1)} %all_to_all.43.own), channel_id=1, source_target_pairs={{0,4},{4,0},{1,5},{5,1},{2,6},{6,2},{3,7},{7,3},{8,12},{12,8},{9,1... | collective-permute-start | bytes 589832 | tf_op jit(solution)/shard_map/ppermute | solution.py:379
  66.3 1.1 collective-permute-done.1.other
  67.3 6.8 %newton.3 = (f32[8,128]{1,0:T(8,128)S(1)}, f32[8,128]{1,0:T(8,128)S(1)}, f32[8,48,128]{2,1,0:T(8,128)S(1)}) custom-call(s32[1,2]{1,0:T(1,128)S(1)} %copy-done.1, s32[128]{0:T(128)S(1)} %copy-done.2, f32[8,48,128]{2,1,0:T(8,128)S(1)} %all_to_all.43.own, f32[8,48,128]{2,1,0:T(8,128)S(1)} %collective-permute-done.1.other, ...), custom_call_target="tpu_custom_call" | custom-call | tf_op jit(solution)/shard_map/newton/pallas_call | solution.py:442
  74.2 8.7 %all_to_all.44.arrived = f32[8,48,128]{2,1,0:T(8,128)S(1)} all-to-all(f32[8,48,128]{2,1,0:T(8,128)S(1)} %get-tuple-element.26), channel_id=1, replica_groups=mesh['y'=4,'z'=8,'core'=2,'cell'=4] {'y','core'}, dimensions={0} | all-to-all | bytes 393216 | tf_op jit(solution)/shard_map/all_to_all | solution.py:383
  82.8 0.7 relay.6
  83.5 3.4 %all-to-all-start.5 = ((f32[8,40,128]{2,1,0:T(8,128)}), f32[8,40,128]{2,1,0:T(8,128)S(1)}, u32[]{:S(2)}, u32[]{:S(2)}) async-start(f32[8,40,128]{2,1,0:T(8,128)} %relay.6), calls=%async_computation.5 | async-start | bytes 327680 | tf_op jit(solution)/shard_map/all_to_all | solution.py:389
  86.9 3.4 %ols.1.control = f32[8,128]{1,0:T(8,128)S(1)} custom-call(f32[8,48,128]{2,1,0:T(8,128)S(1)} %all_to_all.44.arrived, f32[8,128]{1,0:T(8,128)S(1)} %get-tuple-element.27.extras), custom_call_target="tpu_custom_call" | custom-call | flops 8589934592 | bytes 10485760 | tf_op jit(solution)/shard_map/ols/pallas_call | solution.py:451
  90.3 4.6 %all-to-all-done.5.own = f32[8,40,128]{2,1,0:T(8,128)S(1)} async-done(((f32[8,40,128]{2,1,0:T(8,128)}), f32[8,40,128]{2,1,0:T(8,128)S(1)}, u32[]{:S(2)}, u32[]{:S(2)}) %all-to-all-start.5) | async-done | bytes 163872 | tf_op jit(solution)/shard_map/all_to_all | solution.py:389
  94.9 2.6 %collective-permute-start.2 = (f32[8,40,128]{2,1,0:T(8,128)S(1)}, f32[8,40,128]{2,1,0:T(8,128)S(1)}, u32[]{:S(2)}, u32[]{:S(2)}) collective-permute-start(f32[8,40,128]{2,1,0:T(8,128)S(1)} %all-to-all-done.5.own), channel_id=1, source_target_pairs={{0,4},{4,0},{1,5},{5,1},{2,6},{6,2},{3,7},{7,3},{8,12},{12,8},{9,1... | collective-permute-start | bytes 491528 | tf_op jit(solution)/shard_map/ppermute | solution.py:379
  97.5 1.0 collective-permute-done.2.other
  98.5 4.0 %last.1.message.m0 = f32[8,128]{1,0:T(8,128)S(1)} custom-call(s32[1,2]{1,0:T(1,128)S(1)} %copy-done.1, f32[8,40,128]{2,1,0:T(8,128)S(1)} %all-to-all-done.5.own, f32[8,40,128]{2,1,0:T(8,128)S(1)} %collective-permute-done.2.other, f32[8,128]{1,0:T(8,128)S(1)} %ols.1.control, f32[8,128]{1,0:T(8,128)S(1)} %get-tuple-element.30.before, ...), custom_call_target="tpu_custom_call" | custom-call | tf_op jit(solution)/shard_map/last/pallas_call | solution.py:453
  102.6 2.6 %collective-permute-start.5 = (f32[8,128]{1,0:T(8,128)S(1)}, f32[8,128]{1,0:T(8,128)S(1)}, u32[]{:S(2)}, u32[]{:S(2)}) collective-permute-start(f32[8,128]{1,0:T(8,128)S(1)} %last.1.message.m0), channel_id=1, source_target_pairs={{0,3},{1,2},{2,1},{3,0},{4,7},{5,6},{6,5},{7,4},{8,11},{9,10},{10,... | collective-permute-start | bytes 12296 | tf_op jit(solution)/shard_map/ppermute | solution.py:469
  105.1 0.5 collective-permute-start.4
  105.7 0.2 collective-permute-start.3
  105.9 3.7 %bring.1 = (bf16[128,16384]{1,0:T(8,128)(2,1)S(1)}, f32[8,16384]{1,0:T(8,128)S(1)}, bf16[16384,128]{1,0:T(8,128)(2,1)S(1)}) custom-call(f32[8,128]{1,0:T(8,128)S(1)} %last.1.message.m0, bf16[128,16384]{1,0:T(8,128)(2,1)} %get-tuple-element.32.xt_hbm, f32[8,16384]{1,0:T(8,128)} %y_hbm.3, bf16[16384,128]{1,0:T(8,128)(2,1)} %mult_hbm.1), custom_call_target="tpu_custom_call" | custom-call | flops 8589934592 | bytes 10485760 | tf_op jit(solution)/shard_map/bring/pallas_call | solution.py:456
  109.6 0.0 collective-permute-done.5.m3
  109.6 0.0 collective-permute-done.4.m2
  109.6 0.0 collective-permute-done.3.m1
  109.6 2.0 %draws.1 = (f32[8,16,128]{2,1,0:T(8,128)S(1)}, f32[1,16384]{1,0:T(1,128)S(1)}, f32[1,16384]{1,0:T(1,128)S(1)}, f32[1,16384]{1,0:T(1,128)S(1)}) custom-call(s32[128]{0:T(128)S(1)} %copy-done.2, f32[8,128]{1,0:T(8,128)S(1)} %last.1.message.m0, f32[8,128]{1,0:T(8,128)S(1)} %collective-permute-done.3.m1, f32[8,128]{1,0:T(8,128)S(1)} %collective-permute-done.4.m2, ...), custom_call_target="tpu_custom_call" | custom-call | tf_op jit(solution)/shard_map/draws/pallas_call | solution.py:471
  111.6 8.5 %all_to_all.45.arrived = f32[8,16,128]{2,1,0:T(8,128)S(1)} all-to-all(f32[8,16,128]{2,1,0:T(8,128)S(1)} %get-tuple-element.36), channel_id=1, replica_groups=mesh['y'=4,'z'=8,'core'=2,'cell'=4] {'y','core'}, dimensions={0} | all-to-all | bytes 131072 | tf_op jit(solution)/shard_map/all_to_all | solution.py:383
  120.2 9.7 %all_to_all.46.arrived = f32[8,16,128]{2,1,0:T(8,128)S(1)} all-to-all(f32[8,16,128]{2,1,0:T(8,128)S(1)} %relay.7), channel_id=1, replica_groups=mesh['y'=4,'z'=8,'core'=2,'cell'=4] {'z'}, dimensions={0} | all-to-all | bytes 131072 | tf_op jit(solution)/shard_map/all_to_all | solution.py:389
  129.9 0.8 finish.1
  (9 shorter events, 0.1 us)
Async XLA Ops:
  0.6 34.6 %copy-start.1 = (s32[1,2]{1,0:T(1,128)S(1)}, s32[1,2]{1,0:T(1,128)}, u32[]{:S(2)}) copy-start(s32[1,2]{1,0:T(1,128)} %cells.7) | copy-start | bytes 28
  0.6 34.6 %copy-start.2 = (s32[128]{0:T(128)S(1)}, s32[128]{0:T(128)}, u32[]{:S(2)}) copy-start(s32[128]{0:T(128)} %cohorts.7) | copy-start | bytes 1540
  0.6 34.6 %copy-start = (f32[8,16384]{1,0:T(8,128)S(1)}, f32[8,16384]{1,0:T(8,128)}, u32[]{:S(2)}) copy-start(f32[8,16384]{1,0:T(8,128)} %y_hbm.3) | copy-start | bytes 1572868
  32.6 4.7 %collective-permute-start = (f32[8,40,128]{2,1,0:T(8,128)S(1)}, f32[8,40,128]{2,1,0:T(8,128)S(1)}, u32[]{:S(2)}, u32[]{:S(2)}) collective-permute-start(f32[8,40,128]{2,1,0:T(8,128)S(1)} %all_to_all.41.own), channel_id=1, source_target_pairs={{0,4},{4,0},{1,5},{5,1},{2,6},{6,2},{3,7},{7,3},{8,12},{12,8},{9,1... | collective-permute-start | bytes 491528 | tf_op jit(solution)/shard_map/ppermute | solution.py:379
  63.5 3.9 %collective-permute-start.1 = (f32[8,48,128]{2,1,0:T(8,128)S(1)}, f32[8,48,128]{2,1,0:T(8,128)S(1)}, u32[]{:S(2)}, u32[]{:S(2)}) collective-permute-start(f32[8,48,128]{2,1,0:T(8,128)S(1)} %all_to_all.43.own), channel_id=1, source_target_pairs={{0,4},{4,0},{1,5},{5,1},{2,6},{6,2},{3,7},{7,3},{8,12},{12,8},{9,1... | collective-permute-start | bytes 589832 | tf_op jit(solution)/shard_map/ppermute | solution.py:379
  83.5 11.4 %all-to-all-start.5 = ((f32[8,40,128]{2,1,0:T(8,128)}), f32[8,40,128]{2,1,0:T(8,128)S(1)}, u32[]{:S(2)}, u32[]{:S(2)}) async-start(f32[8,40,128]{2,1,0:T(8,128)} %relay.6), calls=%async_computation.5 | async-start | bytes 327680 | tf_op jit(solution)/shard_map/all_to_all | solution.py:389
  94.9 3.6 %collective-permute-start.2 = (f32[8,40,128]{2,1,0:T(8,128)S(1)}, f32[8,40,128]{2,1,0:T(8,128)S(1)}, u32[]{:S(2)}, u32[]{:S(2)}) collective-permute-start(f32[8,40,128]{2,1,0:T(8,128)S(1)} %all-to-all-done.5.own), channel_id=1, source_target_pairs={{0,4},{4,0},{1,5},{5,1},{2,6},{6,2},{3,7},{7,3},{8,12},{12,8},{9,1... | collective-permute-start | bytes 491528 | tf_op jit(solution)/shard_map/ppermute | solution.py:379
  102.6 7.0 %collective-permute-start.5 = (f32[8,128]{1,0:T(8,128)S(1)}, f32[8,128]{1,0:T(8,128)S(1)}, u32[]{:S(2)}, u32[]{:S(2)}) collective-permute-start(f32[8,128]{1,0:T(8,128)S(1)} %last.1.message.m0), channel_id=1, source_target_pairs={{0,3},{1,2},{2,1},{3,0},{4,7},{5,6},{6,5},{7,4},{8,11},{9,10},{10,... | collective-permute-start | bytes 12296 | tf_op jit(solution)/shard_map/ppermute | solution.py:469
  105.1 4.4 %collective-permute-start.4 = (f32[8,128]{1,0:T(8,128)S(1)}, f32[8,128]{1,0:T(8,128)S(1)}, u32[]{:S(2)}, u32[]{:S(2)}) collective-permute-start(f32[8,128]{1,0:T(8,128)S(1)} %last.1.message.m0), channel_id=1, source_target_pairs={{0,2},{1,3},{2,0},{3,1},{4,6},{5,7},{6,4},{7,5},{8,10},{9,11},{10,... | collective-permute-start | bytes 12296 | tf_op jit(solution)/shard_map/ppermute | solution.py:469
  105.7 3.9 %collective-permute-start.3 = (f32[8,128]{1,0:T(8,128)S(1)}, f32[8,128]{1,0:T(8,128)S(1)}, u32[]{:S(2)}, u32[]{:S(2)}) collective-permute-start(f32[8,128]{1,0:T(8,128)S(1)} %last.1.message.m0), channel_id=1, source_target_pairs={{0,1},{1,0},{2,3},{3,2},{4,5},{5,4},{6,7},{7,6},{8,9},{9,8},{10,11... | collective-permute-start | bytes 12296 | tf_op jit(solution)/shard_map/ppermute | solution.py:469

commit v2 on v1

--- a/solution.py
+++ b/solution.py
@@ -150,7 +150,7 @@
 
 
 def first_kernel(
-    cells_hbm, cohorts_hbm, x_hbm, y_hbm, x, xt, xt_hbm, out, cells, cohorts, y, x_sems, y_sems, xt_sems, sems
+    cells_hbm, cohorts_hbm, x_hbm, y_hbm, x, xt, out, cells, cohorts, y, x_sems, y_sems, sems
 ):
     per = CHUNK // WIDTH
     small = [
@@ -166,15 +166,11 @@
     group, period = cells[0, 0], cells[0, 1]
     total = jnp.zeros((WIDTH + 16, WIDTH), F32)
     changes = jnp.zeros((1, WIDTH), F32)
-    sent = []
     for i, copy in enumerate(x_copies):
         copy.wait()
         here = x[chunk_of(i), :]
         turned = here.T
         xt[:, chunk_of(i)] = turned
-        span = pl.ds(i * CHUNK, CHUNK)
-        sent.append(pltpu.make_async_copy(xt.at[:, span], xt_hbm.at[:, span], xt_sems.at[i]))
-        sent[-1].start()
         left, marks = [], []
         for b in range(per):
             cohort = cohorts[i * per + b]
@@ -193,8 +189,6 @@
     scalar = jnp.sum(changes, axis=1, keepdims=True)
     first_lane = iota((1, WIDTH), 1) == 0
     write_payload(out, folded, (total[WIDTH : WIDTH + 1], jnp.where(first_lane, scalar, diagonal)))
-    for copy in sent:
-        copy.wait()
 
 
 def control_kernel(cells, cohorts, x, xt, y, out):
@@ -291,14 +285,14 @@
     )
 
 
-def bring_kernel(message, xt_hbm, y_hbm, mult_hbm, xt, y, mult, xt_sems, y_sems, mult_sems):
-    copies = arrivals(xt_hbm, xt, xt_sems, 1) + arrivals(y_hbm, y, y_sems, 1)
+def bring_kernel(message, x_hbm, y_hbm, mult_hbm, x, y, mult, x_sems, y_sems, mult_sems):
+    copies = arrivals(x_hbm, x, x_sems, 0) + arrivals(y_hbm, y, y_sems, 1)
     for copy in copies + arrivals(mult_hbm, mult, mult_sems, 0):
         copy.wait()
 
 
 def draws_kernel(
-    cohorts, m0, m1, m2, m3, xt, y, mult, out, treated_out, product_out, odds_out
+    cohorts, m0, m1, m2, m3, x, y, mult, out, treated_out, product_out, odds_out
 ):
     per = CHUNK // WIDTH
     blank = jnp.zeros((4, WIDTH), F32)
@@ -316,8 +310,10 @@
     total = jnp.zeros((48, WIDTH), F32)
     odds_sum = jnp.zeros((8, WIDTH), F32)
     product_sum = jnp.zeros((8, WIDTH), F32)
-    for i in range(xt.shape[1] // CHUNK):
-        both = jnp.dot(left, xt[:, chunk_of(i)], preferred_element_type=F32)
+    for i in range(x.shape[0] // CHUNK):
+        both = lax.dot_general(
+            left, x[chunk_of(i), :], (((1,), (1,)), ((), ())), preferred_element_type=F32
+        )
         parts = []
         for b in range(per):
             span = slice(b * WIDTH, (b + 1) * WIDTH)
@@ -410,22 +406,20 @@
     vector = shape(1, rows_here)
     eight = shape(8, WIDTH)
     cost = pl.CostEstimate(flops=1 << 33, bytes_accessed=10 << 20, transcendentals=0)
-    tall, wide, wide_hbm, payload = call(
+    tall, wide, payload = call(
         first_kernel,
         "first",
         [
             shape(rows_here, WIDTH, dtype=BF16),
             shape(WIDTH, rows_here, dtype=BF16),
-            pltpu.HBM((WIDTH, rows_here), BF16),
             shape(pairs, 40, WIDTH),
         ],
         [HBM] * 4,
-        [FREE, FREE, HBM, VMEM],
+        [FREE, FREE, VMEM],
         [
             pltpu.SMEM(cells.shape, jnp.int32),
             pltpu.SMEM(cohorts.shape, jnp.int32),
             pltpu.VMEM(outcomes.shape, F32),
-            sems,
             sems,
             sems,
             pltpu.SemaphoreType.DMA((2,)),
@@ -453,17 +447,17 @@
     message = call(last_kernel, "last", [eight], [SMEM] + [VMEM] * 5)(
         cells, arrived, swap_cores(arrived), ols, coefs, kept[0]
     )[0]
-    wide, deep, mult = call(
+    near, deep, mult = call(
         bring_kernel,
         "bring",
-        [shape(WIDTH, rows_here, dtype=BF16), shape(*outcomes.shape), shape(rows_here, WIDTH, dtype=BF16)],
+        [shape(rows_here, WIDTH, dtype=BF16), shape(*outcomes.shape), shape(rows_here, WIDTH, dtype=BF16)],
         [VMEM] + [HBM] * 3,
         [FREE] * 3,
         [sems, sems, sems],
         cost,
     )(
         message,
-        *(pltpu.with_memory_space_constraint(v, pltpu.HBM) for v in (wide_hbm, outcomes, multipliers)),
+        *(pltpu.with_memory_space_constraint(v, pltpu.HBM) for v in (covariates, outcomes, multipliers)),
     )
     messages = [message] + [
         lax.ppermute(message, "cell", [(i, i ^ s) for i in range(4)]) for s in range(1, 4)
@@ -473,7 +467,7 @@
         "draws",
         [shape(pairs, 16, WIDTH), vector, vector, vector],
         [SMEM] + [VMEM] * 4 + [FREE] * 3,
-    )(cohorts, *messages, wide, deep, mult)
+    )(cohorts, *messages, near, deep, mult)
     arrived = to_line(to_pairs(payload), 16)
     return call(
         functools.partial(finish_kernel, total_rows),

time: 131 us -> 131 us (level)
  no operation moved by 1% of the time
where the time goes in v2:
time: 131 us; the launch traced here: 130 us
  blocking collectives  73.6 us (56%)
  Pallas kernels  34.6 us (26%)
  starting transfers between devices  14.8 us (11%)
  waiting for transfers between devices  6.72 us (5%)
    all_to_all x4, blocking collectives, to_pairs(): return lax.all_to_all(payload, ('y', 'core'), 0, 0)  36.8 us
    all_to_all x3, blocking collectives, to_line(): return lax.all_to_all(copies[0], 'z', 0, 0)  36.7 us
    pallas_call x2, Pallas kernels, shards(): call(functools.partial(newton_kernel, step == 0), 'newton', [eight, eight...  13.6 us
    ppermute x3, starting transfers between devices, swap_cores(): return lax.ppermute(value, 'core', [(0, 1), (1, 0)])  8.04 us
    all_to_all x1, waiting for transfers between devices, to_line(): return lax.all_to_all(copies[0], 'z', 0, 0)  4.61 us
    pallas_call x1, Pallas kernels, shards(): call(last_kernel, 'last', [eight], [SMEM] + [VMEM] * 5)  4.01 us
    pallas_call x1, Pallas kernels, shards(): call(first_kernel, 'first', [shape(rows_here, WIDTH, dtype=BF16), shape(W...  3.85 us
    pallas_call x1, Pallas kernels, shards(): call(bring_kernel, 'bring', [shape(rows_here, WIDTH, dtype=BF16), shape(*...  3.66 us
  transfers between devices with their start and end apart: 7, of which 3 were waited for; matrix products, arithmetic and copies ran while one was open for 0% of the time, Pallas kernels for 7%

profile of v2, /device:TPU:1, one launch (start us, length us, event | category | flops | bytes accessed | tf_op | source)
XLA Modules:
  0.0 130.4 jit_solution(3658797089411276342)
XLA Ops:
  0.6 0.0 copy-start
  0.7 3.9 %first.1 = (bf16[16384,128]{1,0:T(8,128)(2,1)S(1)}, bf16[128,16384]{1,0:T(8,128)(2,1)S(1)}, f32[8,40,128]{2,1,0:T(8,128)S(1)}) custom-call(s32[1,2]{1,0:T(1,128)} %cells.7, s32[128]{0:T(128)} %cohorts.7, bf16[16384,128]{1,0:T(8,128)(2,1)} %x_hbm.3, f32[8,16384]{1,0:T(8,128)} %y_hbm.3), custom_call_target="tpu_custom_call" | custom-call | tf_op jit(solution)/shard_map/first/pallas_call | solution.py:409
  4.5 11.4 %all_to_all.40.arrived = f32[8,40,128]{2,1,0:T(8,128)S(1)} all-to-all(f32[8,40,128]{2,1,0:T(8,128)S(1)} %get-tuple-element.20), channel_id=1, replica_groups=mesh['y'=4,'z'=8,'core'=2,'cell'=4] {'y','core'}, dimensions={0} | all-to-all | bytes 327680 | tf_op jit(solution)/shard_map/all_to_all | solution.py:379
  15.9 16.0 %all_to_all.41.own = f32[8,40,128]{2,1,0:T(8,128)S(1)} all-to-all(f32[8,40,128]{2,1,0:T(8,128)S(1)} %relay.4), channel_id=1, replica_groups=mesh['y'=4,'z'=8,'core'=2,'cell'=4] {'z'}, dimensions={0} | all-to-all | bytes 327680 | tf_op jit(solution)/shard_map/all_to_all | solution.py:385
  31.9 2.7 %collective-permute-start = (f32[8,40,128]{2,1,0:T(8,128)S(1)}, f32[8,40,128]{2,1,0:T(8,128)S(1)}, u32[]{:S(2)}, u32[]{:S(2)}) collective-permute-start(f32[8,40,128]{2,1,0:T(8,128)S(1)} %all_to_all.41.own), channel_id=1, source_target_pairs={{0,4},{4,0},{1,5},{5,1},{2,6},{6,2},{3,7},{7,3},{8,12},{12,8},{9,1... | collective-permute-start | bytes 491528 | tf_op jit(solution)/shard_map/ppermute | solution.py:375
  34.6 2.0 %control.1 = f32[72,128]{1,0:T(8,128)S(1)} custom-call(s32[1,2]{1,0:T(1,128)S(1)} %copy-done.1, s32[128]{0:T(128)S(1)} %copy-done.2, bf16[16384,128]{1,0:T(8,128)(2,1)S(1)} %get-tuple-element.21.x, bf16[128,16384]{1,0:T(8,128)(2,1)S(1)} %get-tuple-element.22.xt, f32[8,16384]{1,0:T(8,128)S(1)} %copy-done), custom_call_target="tpu_custom_call" | custom-call | flops 8589934592 | bytes 10485760 | tf_op jit(solution)/shard_map/control/pallas_call | solution.py:430
  36.6 0.0 collective-permute-done.other
  36.6 6.8 %newton.2 = (f32[8,128]{1,0:T(8,128)S(1)}, f32[8,128]{1,0:T(8,128)S(1)}, f32[8,48,128]{2,1,0:T(8,128)S(1)}) custom-call(s32[1,2]{1,0:T(1,128)S(1)} %copy-done.1, s32[128]{0:T(128)S(1)} %copy-done.2, f32[8,40,128]{2,1,0:T(8,128)S(1)} %all_to_all.41.own, f32[8,40,128]{2,1,0:T(8,128)S(1)} %collective-permute-done.other, ...), custom_call_target="tpu_custom_call" | custom-call | tf_op jit(solution)/shard_map/newton/pallas_call | solution.py:436
  43.5 8.3 %all_to_all.42.arrived = f32[8,48,128]{2,1,0:T(8,128)S(1)} all-to-all(f32[8,48,128]{2,1,0:T(8,128)S(1)} %get-tuple-element.23), channel_id=1, replica_groups=mesh['y'=4,'z'=8,'core'=2,'cell'=4] {'y','core'}, dimensions={0} | all-to-all | bytes 393216 | tf_op jit(solution)/shard_map/all_to_all | solution.py:379
  51.8 11.0 %all_to_all.43.own = f32[8,48,128]{2,1,0:T(8,128)S(1)} all-to-all(f32[8,48,128]{2,1,0:T(8,128)S(1)} %relay.5), channel_id=1, replica_groups=mesh['y'=4,'z'=8,'core'=2,'cell'=4] {'z'}, dimensions={0} | all-to-all | bytes 393216 | tf_op jit(solution)/shard_map/all_to_all | solution.py:385
  62.8 2.8 %collective-permute-start.1 = (f32[8,48,128]{2,1,0:T(8,128)S(1)}, f32[8,48,128]{2,1,0:T(8,128)S(1)}, u32[]{:S(2)}, u32[]{:S(2)}) collective-permute-start(f32[8,48,128]{2,1,0:T(8,128)S(1)} %all_to_all.43.own), channel_id=1, source_target_pairs={{0,4},{4,0},{1,5},{5,1},{2,6},{6,2},{3,7},{7,3},{8,12},{12,8},{9,1... | collective-permute-start | bytes 589832 | tf_op jit(solution)/shard_map/ppermute | solution.py:375
  65.6 1.1 collective-permute-done.1.other
  66.7 6.8 %newton.3 = (f32[8,128]{1,0:T(8,128)S(1)}, f32[8,128]{1,0:T(8,128)S(1)}, f32[8,48,128]{2,1,0:T(8,128)S(1)}) custom-call(s32[1,2]{1,0:T(1,128)S(1)} %copy-done.1, s32[128]{0:T(128)S(1)} %copy-done.2, f32[8,48,128]{2,1,0:T(8,128)S(1)} %all_to_all.43.own, f32[8,48,128]{2,1,0:T(8,128)S(1)} %collective-permute-done.1.other, ...), custom_call_target="tpu_custom_call" | custom-call | tf_op jit(solution)/shard_map/newton/pallas_call | solution.py:436
  73.5 8.7 %all_to_all.44.arrived = f32[8,48,128]{2,1,0:T(8,128)S(1)} all-to-all(f32[8,48,128]{2,1,0:T(8,128)S(1)} %get-tuple-element.25), channel_id=1, replica_groups=mesh['y'=4,'z'=8,'core'=2,'cell'=4] {'y','core'}, dimensions={0} | all-to-all | bytes 393216 | tf_op jit(solution)/shard_map/all_to_all | solution.py:379
  82.2 0.7 relay.6
  82.8 3.4 %all-to-all-start.5 = ((f32[8,40,128]{2,1,0:T(8,128)}), f32[8,40,128]{2,1,0:T(8,128)S(1)}, u32[]{:S(2)}, u32[]{:S(2)}) async-start(f32[8,40,128]{2,1,0:T(8,128)} %relay.6), calls=%async_computation.5 | async-start | bytes 327680 | tf_op jit(solution)/shard_map/all_to_all | solution.py:385
  86.2 3.4 %ols.1.control = f32[8,128]{1,0:T(8,128)S(1)} custom-call(f32[8,48,128]{2,1,0:T(8,128)S(1)} %all_to_all.44.arrived, f32[8,128]{1,0:T(8,128)S(1)} %get-tuple-element.26.extras), custom_call_target="tpu_custom_call" | custom-call | flops 8589934592 | bytes 10485760 | tf_op jit(solution)/shard_map/ols/pallas_call | solution.py:445
  89.7 4.6 %all-to-all-done.5.own = f32[8,40,128]{2,1,0:T(8,128)S(1)} async-done(((f32[8,40,128]{2,1,0:T(8,128)}), f32[8,40,128]{2,1,0:T(8,128)S(1)}, u32[]{:S(2)}, u32[]{:S(2)}) %all-to-all-start.5) | async-done | bytes 163872 | tf_op jit(solution)/shard_map/all_to_all | solution.py:385
  94.3 2.6 %collective-permute-start.2 = (f32[8,40,128]{2,1,0:T(8,128)S(1)}, f32[8,40,128]{2,1,0:T(8,128)S(1)}, u32[]{:S(2)}, u32[]{:S(2)}) collective-permute-start(f32[8,40,128]{2,1,0:T(8,128)S(1)} %all-to-all-done.5.own), channel_id=1, source_target_pairs={{0,4},{4,0},{1,5},{5,1},{2,6},{6,2},{3,7},{7,3},{8,12},{12,8},{9,1... | collective-permute-start | bytes 491528 | tf_op jit(solution)/shard_map/ppermute | solution.py:375
  96.9 1.0 collective-permute-done.2.other
  97.9 4.0 %last.1.message.m0 = f32[8,128]{1,0:T(8,128)S(1)} custom-call(s32[1,2]{1,0:T(1,128)S(1)} %copy-done.1, f32[8,40,128]{2,1,0:T(8,128)S(1)} %all-to-all-done.5.own, f32[8,40,128]{2,1,0:T(8,128)S(1)} %collective-permute-done.2.other, f32[8,128]{1,0:T(8,128)S(1)} %ols.1.control, f32[8,128]{1,0:T(8,128)S(1)} %get-tuple-element.29.before, ...), custom_call_target="tpu_custom_call" | custom-call | tf_op jit(solution)/shard_map/last/pallas_call | solution.py:447
  101.9 2.6 %collective-permute-start.5 = (f32[8,128]{1,0:T(8,128)S(1)}, f32[8,128]{1,0:T(8,128)S(1)}, u32[]{:S(2)}, u32[]{:S(2)}) collective-permute-start(f32[8,128]{1,0:T(8,128)S(1)} %last.1.message.m0), channel_id=1, source_target_pairs={{0,3},{1,2},{2,1},{3,0},{4,7},{5,6},{6,5},{7,4},{8,11},{9,10},{10,... | collective-permute-start | bytes 12296 | tf_op jit(solution)/shard_map/ppermute | solution.py:463
  104.5 0.5 collective-permute-start.4
  105.0 0.2 collective-permute-start.3
  105.2 3.7 %bring.1 = (bf16[16384,128]{1,0:T(8,128)(2,1)S(1)}, f32[8,16384]{1,0:T(8,128)S(1)}, bf16[16384,128]{1,0:T(8,128)(2,1)S(1)}) custom-call(f32[8,128]{1,0:T(8,128)S(1)} %last.1.message.m0, bf16[16384,128]{1,0:T(8,128)(2,1)} %x_hbm.3, f32[8,16384]{1,0:T(8,128)} %y_hbm.3, bf16[16384,128]{1,0:T(8,128)(2,1)} %mult_hbm.1), custom_call_target="tpu_custom_call" | custom-call | flops 8589934592 | bytes 10485760 | tf_op jit(solution)/shard_map/bring/pallas_call | solution.py:450
  108.9 0.0 collective-permute-done.5.m3
  108.9 0.0 collective-permute-done.4.m2
  108.9 0.0 collective-permute-done.3.m1
  108.9 2.4 %draws.1 = (f32[8,16,128]{2,1,0:T(8,128)S(1)}, f32[1,16384]{1,0:T(1,128)S(1)}, f32[1,16384]{1,0:T(1,128)S(1)}, f32[1,16384]{1,0:T(1,128)S(1)}) custom-call(s32[128]{0:T(128)S(1)} %copy-done.2, f32[8,128]{1,0:T(8,128)S(1)} %last.1.message.m0, f32[8,128]{1,0:T(8,128)S(1)} %collective-permute-done.3.m1, f32[8,128]{1,0:T(8,128)S(1)} %collective-permute-done.4.m2, ...), custom_call_target="tpu_custom_call" | custom-call | tf_op jit(solution)/shard_map/draws/pallas_call | solution.py:465
  111.4 8.5 %all_to_all.45.arrived = f32[8,16,128]{2,1,0:T(8,128)S(1)} all-to-all(f32[8,16,128]{2,1,0:T(8,128)S(1)} %get-tuple-element.34), channel_id=1, replica_groups=mesh['y'=4,'z'=8,'core'=2,'cell'=4] {'y','core'}, dimensions={0} | all-to-all | bytes 131072 | tf_op jit(solution)/shard_map/all_to_all | solution.py:379
  119.9 9.7 %all_to_all.46.arrived = f32[8,16,128]{2,1,0:T(8,128)S(1)} all-to-all(f32[8,16,128]{2,1,0:T(8,128)S(1)} %relay.7), channel_id=1, replica_groups=mesh['y'=4,'z'=8,'core'=2,'cell'=4] {'z'}, dimensions={0} | all-to-all | bytes 131072 | tf_op jit(solution)/shard_map/all_to_all | solution.py:385
  129.6 0.8 finish.1
  (9 shorter events, 0.1 us)
Async XLA Ops:
  0.6 34.0 %copy-start.1 = (s32[1,2]{1,0:T(1,128)S(1)}, s32[1,2]{1,0:T(1,128)}, u32[]{:S(2)}) copy-start(s32[1,2]{1,0:T(1,128)} %cells.7) | copy-start | bytes 28
  0.6 34.0 %copy-start.2 = (s32[128]{0:T(128)S(1)}, s32[128]{0:T(128)}, u32[]{:S(2)}) copy-start(s32[128]{0:T(128)} %cohorts.7) | copy-start | bytes 1540
  0.6 34.0 %copy-start = (f32[8,16384]{1,0:T(8,128)S(1)}, f32[8,16384]{1,0:T(8,128)}, u32[]{:S(2)}) copy-start(f32[8,16384]{1,0:T(8,128)} %y_hbm.3) | copy-start | bytes 1572868
  31.9 4.7 %collective-permute-start = (f32[8,40,128]{2,1,0:T(8,128)S(1)}, f32[8,40,128]{2,1,0:T(8,128)S(1)}, u32[]{:S(2)}, u32[]{:S(2)}) collective-permute-start(f32[8,40,128]{2,1,0:T(8,128)S(1)} %all_to_all.41.own), channel_id=1, source_target_pairs={{0,4},{4,0},{1,5},{5,1},{2,6},{6,2},{3,7},{7,3},{8,12},{12,8},{9,1... | collective-permute-start | bytes 491528 | tf_op jit(solution)/shard_map/ppermute | solution.py:375
  62.8 3.9 %collective-permute-start.1 = (f32[8,48,128]{2,1,0:T(8,128)S(1)}, f32[8,48,128]{2,1,0:T(8,128)S(1)}, u32[]{:S(2)}, u32[]{:S(2)}) collective-permute-start(f32[8,48,128]{2,1,0:T(8,128)S(1)} %all_to_all.43.own), channel_id=1, source_target_pairs={{0,4},{4,0},{1,5},{5,1},{2,6},{6,2},{3,7},{7,3},{8,12},{12,8},{9,1... | collective-permute-start | bytes 589832 | tf_op jit(solution)/shard_map/ppermute | solution.py:375
  82.8 11.4 %all-to-all-start.5 = ((f32[8,40,128]{2,1,0:T(8,128)}), f32[8,40,128]{2,1,0:T(8,128)S(1)}, u32[]{:S(2)}, u32[]{:S(2)}) async-start(f32[8,40,128]{2,1,0:T(8,128)} %relay.6), calls=%async_computation.5 | async-start | bytes 327680 | tf_op jit(solution)/shard_map/all_to_all | solution.py:385
  94.3 3.6 %collective-permute-start.2 = (f32[8,40,128]{2,1,0:T(8,128)S(1)}, f32[8,40,128]{2,1,0:T(8,128)S(1)}, u32[]{:S(2)}, u32[]{:S(2)}) collective-permute-start(f32[8,40,128]{2,1,0:T(8,128)S(1)} %all-to-all-done.5.own), channel_id=1, source_target_pairs={{0,4},{4,0},{1,5},{5,1},{2,6},{6,2},{3,7},{7,3},{8,12},{12,8},{9,1... | collective-permute-start | bytes 491528 | tf_op jit(solution)/shard_map/ppermute | solution.py:375
  101.9 7.0 %collective-permute-start.5 = (f32[8,128]{1,0:T(8,128)S(1)}, f32[8,128]{1,0:T(8,128)S(1)}, u32[]{:S(2)}, u32[]{:S(2)}) collective-permute-start(f32[8,128]{1,0:T(8,128)S(1)} %last.1.message.m0), channel_id=1, source_target_pairs={{0,3},{1,2},{2,1},{3,0},{4,7},{5,6},{6,5},{7,4},{8,11},{9,10},{10,... | collective-permute-start | bytes 12296 | tf_op jit(solution)/shard_map/ppermute | solution.py:463
  104.5 4.5 %collective-permute-start.4 = (f32[8,128]{1,0:T(8,128)S(1)}, f32[8,128]{1,0:T(8,128)S(1)}, u32[]{:S(2)}, u32[]{:S(2)}) collective-permute-start(f32[8,128]{1,0:T(8,128)S(1)} %last.1.message.m0), channel_id=1, source_target_pairs={{0,2},{1,3},{2,0},{3,1},{4,6},{5,7},{6,4},{7,5},{8,10},{9,11},{10,... | collective-permute-start | bytes 12296 | tf_op jit(solution)/shard_map/ppermute | solution.py:463
  105.0 3.9 %collective-permute-start.3 = (f32[8,128]{1,0:T(8,128)S(1)}, f32[8,128]{1,0:T(8,128)S(1)}, u32[]{:S(2)}, u32[]{:S(2)}) collective-permute-start(f32[8,128]{1,0:T(8,128)S(1)} %last.1.message.m0), channel_id=1, source_target_pairs={{0,1},{1,0},{2,3},{3,2},{4,5},{5,4},{6,7},{7,6},{8,9},{9,8},{10,11... | collective-permute-start | bytes 12296 | tf_op jit(solution)/shard_map/ppermute | solution.py:463

commit v3 on v2

--- a/solution.py
+++ b/solution.py
@@ -14,7 +14,6 @@
 WIDTH = 128
 HALF = 64
 CHUNK = 4096
-PACKED = 40
 VMEM = pl.BlockSpec(memory_space=pltpu.VMEM)
 SMEM = pl.BlockSpec(memory_space=pltpu.SMEM)
 HBM = pl.BlockSpec(memory_space=pltpu.HBM)
@@ -51,12 +50,28 @@
     return top, jnp.where(col < HALF, turned[HALF:], low)
 
 
-def write_payload(out, folded, extras):
-    pad = jnp.zeros((7, WIDTH), F32)
+def packed(rows):
+    spots = [(i, i + 17) for i in range(17)] + [(i, i + 5) for i in range(34, rows.shape[0] - 5)]
+    return jnp.concatenate(
+        [jnp.concatenate([rows[i : i + 1], rows[j : j + 1]], axis=0) for i, j in spots], axis=1
+    )
+
+
+def unpacked(value, first, count):
+    rows = []
+    for i in range(first, first + count):
+        part, spot = divmod(i, 17) if i < 34 else divmod(i - 34, 5)
+        spot = spot + 17 if i >= 34 else spot
+        rows.append(value[part : part + 1, spot * WIDTH : (spot + 1) * WIDTH])
+    return jnp.concatenate(rows, axis=0)
+
+
+def write_payload(out, folded, extras, more=None):
     for p in range(out.shape[0]):
         h = p % 2
-        out[p, 0:32, :] = folded[32 * h : 32 * h + 32]
-        out[p, 32:40, :] = jnp.concatenate([extras[h], pad], axis=0)
+        rows = [folded[32 * h : 32 * h + 32], extras[h], jnp.zeros((1, WIDTH), F32)]
+        rows += [more[p]] if more else []
+        out[p] = packed(jnp.concatenate(rows, axis=0))
 
 
 def summed(ref):
@@ -219,13 +234,14 @@
     group, period = cells[0, 0], cells[0, 1]
     per = CHUNK // WIDTH
     mine = summed(own)
-    folded, row, diagonal = halves(lax.axis_index("core"), mine[:40], summed(other)[:40])
+    core = lax.axis_index("core")
+    folded, row, diagonal = halves(core, unpacked(mine, 0, 33), unpacked(summed(other), 0, 33))
     top, low = unfold(folded, diagonal)
     if first:
         keep[...] = jnp.concatenate([row, diagonal, jnp.zeros((6, WIDTH), F32)], axis=0)
         new = 4.0 * solve(top, low, row - 0.5 * top[0:1])
     else:
-        keep[...] = mine[32:40]
+        keep[...] = jnp.concatenate([unpacked(mine, 34, 2), jnp.zeros((6, WIDTH), F32)], axis=0)
         new = before[...] + solve(top, low, row)
     coefs[...] = new
     rounded = jnp.concatenate([new, new], axis=0).astype(BF16)
@@ -248,23 +264,26 @@
         left = jnp.concatenate([jnp.concatenate(left, axis=1), jnp.concatenate(errors, axis=1)], axis=0)
         total = total + jnp.dot(left, x[chunk_of(i), :], preferred_element_type=F32)
     folded, diagonal = fold(total[:WIDTH])
-    write_payload(out, folded, (total[WIDTH : WIDTH + 1], diagonal))
-    for p in range(out.shape[0]):
-        if first:
-            out[p, 33:35, :] = control[64:66, :]
-            out[p, 40:48, :] = control[8 * p : 8 * p + 8, :]
-        else:
-            out[p, 40:48, :] = mine[40:48]
+    if first:
+        more = [
+            jnp.concatenate([control[64:66, :], control[8 * p : 8 * p + 8, :]], axis=0)
+            for p in range(out.shape[0])
+        ]
+    else:
+        piece = jnp.concatenate([jnp.zeros((2, WIDTH), F32), unpacked(mine, 36, 8)], axis=0)
+        more = [piece] * out.shape[0]
+    write_payload(out, folded, (total[WIDTH : WIDTH + 1], diagonal), more)
 
 
 def control_solve_kernel(arrived, extras, out):
-    folded = jnp.concatenate([arrived[p, 40:48, :] for p in range(arrived.shape[0])], axis=0)
-    solved = solve(*unfold(folded, extras[2:3, :]), extras[1:2, :])
+    folded = jnp.concatenate([unpacked(arrived[p], 36, 8) for p in range(arrived.shape[0])], axis=0)
+    solved = solve(*unfold(folded, extras[1:2, :]), extras[0:1, :])
     out[...] = solved.astype(BF16).astype(F32)
 
 
 def last_kernel(cells, own, other, control, before, keep, out):
-    folded, row, diagonal = halves(lax.axis_index("core"), summed(own), summed(other))
+    core = lax.axis_index("core")
+    folded, row, diagonal = halves(core, unpacked(summed(own), 0, 33), unpacked(summed(other), 0, 33))
     new = before[...] + solve(*unfold(folded, diagonal), row)
     ols = control[0:1, :]
     treated_x = keep[0:1, :]
@@ -353,8 +372,7 @@
 
 
 def relay_kernel(arrived, out):
-    rows = out.shape[1]
-    total = summed(arrived)[:rows]
+    total = summed(arrived)[:, : out.shape[2]]
     for p in range(out.shape[0]):
         out[p] = total
 
@@ -379,9 +397,9 @@
     return lax.all_to_all(payload, ("y", "core"), 0, 0)
 
 
-def to_line(arrived, rows):
+def to_line(arrived, size):
     peers = lax.axis_size("z")
-    copies = call(relay_kernel, "relay", [shape(peers, rows, WIDTH)], [VMEM])(arrived)
+    copies = call(relay_kernel, "relay", [shape(peers, arrived.shape[1], size)], [VMEM])(arrived)
     return lax.all_to_all(copies[0], "z", 0, 0)
 
 
@@ -412,7 +430,7 @@
         [
             shape(rows_here, WIDTH, dtype=BF16),
             shape(WIDTH, rows_here, dtype=BF16),
-            shape(pairs, 40, WIDTH),
+            shape(pairs, 2, 17 * WIDTH),
         ],
         [HBM] * 4,
         [FREE, FREE, VMEM],
@@ -426,7 +444,7 @@
         ],
     )(*(pltpu.with_memory_space_constraint(v, pltpu.HBM) for v in (cells, cohorts, covariates, outcomes)))
     halfway = to_pairs(payload)
-    arrived = to_line(halfway, 40)
+    arrived = to_line(halfway, 17 * WIDTH)
     control = call(
         control_kernel, "control", [shape(72, WIDTH)], [SMEM, SMEM, FREE, FREE, FREE], cost=cost
     )(cells, cohorts, tall, wide, outcomes)[0]
@@ -436,12 +454,12 @@
         coefs, keep, payload = call(
             functools.partial(newton_kernel, step == 0),
             "newton",
-            [eight, eight, shape(pairs, 48, WIDTH)],
+            [eight, eight, shape(pairs, 2, 22 * WIDTH)],
             [SMEM, SMEM, VMEM, VMEM, FREE, FREE, VMEM, VMEM],
         )(cells, cohorts, arrived, swap_cores(arrived), tall, wide, coefs, control)
         kept.append(keep)
         halfway = to_pairs(payload)
-        arrived = to_line(halfway, 48 if step == 0 else 40)
+        arrived = to_line(halfway, (22 - 5 * step) * WIDTH)
     ols = call(control_solve_kernel, "ols", [eight], [VMEM, VMEM], cost=cost)(halfway, kept[1])[0]
     arrived, ols = lax.optimization_barrier((arrived, ols))
     message = call(last_kernel, "last", [eight], [SMEM] + [VMEM] * 5)(
@@ -468,7 +486,7 @@
         [shape(pairs, 16, WIDTH), vector, vector, vector],
         [SMEM] + [VMEM] * 4 + [FREE] * 3,
     )(cohorts, *messages, near, deep, mult)
-    arrived = to_line(to_pairs(payload), 16)
+    arrived = to_line(to_pairs(payload), WIDTH)
     return call(
         functools.partial(finish_kernel, total_rows),
         "finish",

time: 131 us -> 129 us (0.985)
  no operation moved by 1% of the time
where the time goes in v3:
time: 129 us
  blocking collectives  72.6 us (56%)
  Pallas kernels  34.7 us (27%)
  starting transfers between devices  14.2 us (11%)
  waiting for transfers between devices  6.36 us (5%)
    all_to_all x3, blocking collectives, to_line(): return lax.all_to_all(copies[0], 'z', 0, 0)  36.4 us
    all_to_all x4, blocking collectives, to_pairs(): return lax.all_to_all(payload, ('y', 'core'), 0, 0)  36.3 us
    pallas_call x2, Pallas kernels, shards(): call(functools.partial(newton_kernel, step == 0), 'newton', [eight, eight...  13.7 us
    ppermute x3, starting transfers between devices, swap_cores(): return lax.ppermute(value, 'core', [(0, 1), (1, 0)])  7.45 us
    all_to_all x1, waiting for transfers between devices, to_line(): return lax.all_to_all(copies[0], 'z', 0, 0)  4.3 us
    pallas_call x1, Pallas kernels, shards(): call(last_kernel, 'last', [eight], [SMEM] + [VMEM] * 5)  4.03 us
    pallas_call x1, Pallas kernels, shards(): call(first_kernel, 'first', [shape(rows_here, WIDTH, dtype=BF16), shape(W...  3.86 us
    pallas_call x1, Pallas kernels, shards(): call(bring_kernel, 'bring', [shape(rows_here, WIDTH, dtype=BF16), shape(*...  3.66 us
  transfers between devices with their start and end apart: 7, of which 3 were waited for; matrix products, arithmetic and copies ran while one was open for 0% of the time, Pallas kernels for 7%

profile of v3, /device:TPU:1, one launch (start us, length us, event | category | flops | bytes accessed | tf_op | source)
XLA Modules:
  0.0 128.6 jit_solution(10730569847075584753)
XLA Ops:
  0.6 0.0 copy-start
  0.7 3.9 %first.1 = (bf16[16384,128]{1,0:T(8,128)(2,1)S(1)}, bf16[128,16384]{1,0:T(8,128)(2,1)S(1)}, f32[8,2,2176]{2,1,0:T(2,128)S(1)}) custom-call(s32[1,2]{1,0:T(1,128)} %cells.7, s32[128]{0:T(128)} %cohorts.7, bf16[16384,128]{1,0:T(8,128)(2,1)} %x_hbm.3, f32[8,16384]{1,0:T(8,128)} %y_hbm.3), custom_call_target="tpu_custom_call" | custom-call | tf_op jit(solution)/shard_map/first/pallas_call | solution.py:427
  4.5 11.1 %all_to_all.40.arrived = f32[8,2,2176]{2,1,0:T(2,128)S(1)} all-to-all(f32[8,2,2176]{2,1,0:T(2,128)S(1)} %get-tuple-element.20), channel_id=1, replica_groups=mesh['y'=4,'z'=8,'core'=2,'cell'=4] {'y','core'}, dimensions={0} | all-to-all | bytes 278528 | tf_op jit(solution)/shard_map/all_to_all | solution.py:397
  15.7 15.8 %all_to_all.41.own = f32[8,2,2176]{2,1,0:T(2,128)S(1)} all-to-all(f32[8,2,2176]{2,1,0:T(2,128)S(1)} %relay.4), channel_id=1, replica_groups=mesh['y'=4,'z'=8,'core'=2,'cell'=4] {'z'}, dimensions={0} | all-to-all | bytes 278528 | tf_op jit(solution)/shard_map/all_to_all | solution.py:403
  31.5 2.5 %collective-permute-start = (f32[8,2,2176]{2,1,0:T(2,128)S(1)}, f32[8,2,2176]{2,1,0:T(2,128)S(1)}, u32[]{:S(2)}, u32[]{:S(2)}) collective-permute-start(f32[8,2,2176]{2,1,0:T(2,128)S(1)} %all_to_all.41.own), channel_id=1, source_target_pairs={{0,4},{4,0},{1,5},{5,1},{2,6},{6,2},{3,7},{7,3},{8,12},{12,8},{9,1... | collective-permute-start | bytes 417800 | tf_op jit(solution)/shard_map/ppermute | solution.py:393
  34.0 2.0 %control.1 = f32[72,128]{1,0:T(8,128)S(1)} custom-call(s32[1,2]{1,0:T(1,128)S(1)} %copy-done.1, s32[128]{0:T(128)S(1)} %copy-done.2, bf16[16384,128]{1,0:T(8,128)(2,1)S(1)} %get-tuple-element.21.x, bf16[128,16384]{1,0:T(8,128)(2,1)S(1)} %get-tuple-element.22.xt, f32[8,16384]{1,0:T(8,128)S(1)} %copy-done), custom_call_target="tpu_custom_call" | custom-call | flops 8589934592 | bytes 10485760 | tf_op jit(solution)/shard_map/control/pallas_call | solution.py:448
  36.0 0.0 collective-permute-done.other
  36.0 6.9 %newton.2 = (f32[8,128]{1,0:T(8,128)S(1)}, f32[8,128]{1,0:T(8,128)S(1)}, f32[8,2,2816]{2,1,0:T(2,128)S(1)}) custom-call(s32[1,2]{1,0:T(1,128)S(1)} %copy-done.1, s32[128]{0:T(128)S(1)} %copy-done.2, f32[8,2,2176]{2,1,0:T(2,128)S(1)} %all_to_all.41.own, f32[8,2,2176]{2,1,0:T(2,128)S(1)} %collective-permute-done.other, ...), custom_call_target="tpu_custom_call" | custom-call | tf_op jit(solution)/shard_map/newton/pallas_call | solution.py:454
  42.9 8.1 %all_to_all.42.arrived = f32[8,2,2816]{2,1,0:T(2,128)S(1)} all-to-all(f32[8,2,2816]{2,1,0:T(2,128)S(1)} %get-tuple-element.23), channel_id=1, replica_groups=mesh['y'=4,'z'=8,'core'=2,'cell'=4] {'y','core'}, dimensions={0} | all-to-all | bytes 360448 | tf_op jit(solution)/shard_map/all_to_all | solution.py:397
  51.0 10.9 %all_to_all.43.own = f32[8,2,2816]{2,1,0:T(2,128)S(1)} all-to-all(f32[8,2,2816]{2,1,0:T(2,128)S(1)} %relay.5), channel_id=1, replica_groups=mesh['y'=4,'z'=8,'core'=2,'cell'=4] {'z'}, dimensions={0} | all-to-all | bytes 360448 | tf_op jit(solution)/shard_map/all_to_all | solution.py:403
  61.9 2.6 %collective-permute-start.1 = (f32[8,2,2816]{2,1,0:T(2,128)S(1)}, f32[8,2,2816]{2,1,0:T(2,128)S(1)}, u32[]{:S(2)}, u32[]{:S(2)}) collective-permute-start(f32[8,2,2816]{2,1,0:T(2,128)S(1)} %all_to_all.43.own), channel_id=1, source_target_pairs={{0,4},{4,0},{1,5},{5,1},{2,6},{6,2},{3,7},{7,3},{8,12},{12,8},{9,1... | collective-permute-start | bytes 540680 | tf_op jit(solution)/shard_map/ppermute | solution.py:393
  64.5 1.0 collective-permute-done.1.other
  65.6 6.9 %newton.3 = (f32[8,128]{1,0:T(8,128)S(1)}, f32[8,128]{1,0:T(8,128)S(1)}, f32[8,2,2816]{2,1,0:T(2,128)S(1)}) custom-call(s32[1,2]{1,0:T(1,128)S(1)} %copy-done.1, s32[128]{0:T(128)S(1)} %copy-done.2, f32[8,2,2816]{2,1,0:T(2,128)S(1)} %all_to_all.43.own, f32[8,2,2816]{2,1,0:T(2,128)S(1)} %collective-permute-done.1.other, ...), custom_call_target="tpu_custom_call" | custom-call | tf_op jit(solution)/shard_map/newton/pallas_call | solution.py:454
  72.4 8.5 %all_to_all.44.arrived = f32[8,2,2816]{2,1,0:T(2,128)S(1)} all-to-all(f32[8,2,2816]{2,1,0:T(2,128)S(1)} %get-tuple-element.25), channel_id=1, replica_groups=mesh['y'=4,'z'=8,'core'=2,'cell'=4] {'y','core'}, dimensions={0} | all-to-all | bytes 360448 | tf_op jit(solution)/shard_map/all_to_all | solution.py:397
  80.9 0.7 relay.6
  81.6 3.4 %all-to-all-start.5 = ((f32[8,2,2176]{2,1,0:T(2,128)}), f32[8,2,2176]{2,1,0:T(2,128)S(1)}, u32[]{:S(2)}, u32[]{:S(2)}) async-start(f32[8,2,2176]{2,1,0:T(2,128)} %relay.6), calls=%async_computation.5 | async-start | bytes 278528 | tf_op jit(solution)/shard_map/all_to_all | solution.py:403
  85.0 3.4 %ols.1.control = f32[8,128]{1,0:T(8,128)S(1)} custom-call(f32[8,2,2816]{2,1,0:T(2,128)S(1)} %all_to_all.44.arrived, f32[8,128]{1,0:T(8,128)S(1)} %get-tuple-element.26.extras), custom_call_target="tpu_custom_call" | custom-call | flops 8589934592 | bytes 10485760 | tf_op jit(solution)/shard_map/ols/pallas_call | solution.py:463
  88.4 4.3 %all-to-all-done.5.own = f32[8,2,2176]{2,1,0:T(2,128)S(1)} async-done(((f32[8,2,2176]{2,1,0:T(2,128)}), f32[8,2,2176]{2,1,0:T(2,128)S(1)}, u32[]{:S(2)}, u32[]{:S(2)}) %all-to-all-start.5) | async-done | bytes 139296 | tf_op jit(solution)/shard_map/all_to_all | solution.py:403
  92.7 2.4 %collective-permute-start.2 = (f32[8,2,2176]{2,1,0:T(2,128)S(1)}, f32[8,2,2176]{2,1,0:T(2,128)S(1)}, u32[]{:S(2)}, u32[]{:S(2)}) collective-permute-start(f32[8,2,2176]{2,1,0:T(2,128)S(1)} %all-to-all-done.5.own), channel_id=1, source_target_pairs={{0,4},{4,0},{1,5},{5,1},{2,6},{6,2},{3,7},{7,3},{8,12},{12,8},{9,1... | collective-permute-start | bytes 417800 | tf_op jit(solution)/shard_map/ppermute | solution.py:393
  95.1 1.0 collective-permute-done.2.other
  96.1 4.0 %last.1.message.m0 = f32[8,128]{1,0:T(8,128)S(1)} custom-call(s32[1,2]{1,0:T(1,128)S(1)} %copy-done.1, f32[8,2,2176]{2,1,0:T(2,128)S(1)} %all-to-all-done.5.own, f32[8,2,2176]{2,1,0:T(2,128)S(1)} %collective-permute-done.2.other, f32[8,128]{1,0:T(8,128)S(1)} %ols.1.control, f32[8,128]{1,0:T(8,128)S(1)} %get-tuple-element.29.before, ...), custom_call_target="tpu_custom_call" | custom-call | tf_op jit(solution)/shard_map/last/pallas_call | solution.py:465
  100.1 2.6 %collective-permute-start.5 = (f32[8,128]{1,0:T(8,128)S(1)}, f32[8,128]{1,0:T(8,128)S(1)}, u32[]{:S(2)}, u32[]{:S(2)}) collective-permute-start(f32[8,128]{1,0:T(8,128)S(1)} %last.1.message.m0), channel_id=1, source_target_pairs={{0,3},{1,2},{2,1},{3,0},{4,7},{5,6},{6,5},{7,4},{8,11},{9,10},{10,... | collective-permute-start | bytes 12296 | tf_op jit(solution)/shard_map/ppermute | solution.py:481
  102.7 0.5 collective-permute-start.4
  103.2 0.3 collective-permute-start.3
  103.5 3.7 %bring.1 = (bf16[16384,128]{1,0:T(8,128)(2,1)S(1)}, f32[8,16384]{1,0:T(8,128)S(1)}, bf16[16384,128]{1,0:T(8,128)(2,1)S(1)}) custom-call(f32[8,128]{1,0:T(8,128)S(1)} %last.1.message.m0, bf16[16384,128]{1,0:T(8,128)(2,1)} %x_hbm.3, f32[8,16384]{1,0:T(8,128)} %y_hbm.3, bf16[16384,128]{1,0:T(8,128)(2,1)} %mult_hbm.1), custom_call_target="tpu_custom_call" | custom-call | flops 8589934592 | bytes 10485760 | tf_op jit(solution)/shard_map/bring/pallas_call | solution.py:468
  107.1 0.0 collective-permute-done.5.m3
  107.1 0.0 collective-permute-done.4.m2
  107.1 0.0 collective-permute-done.3.m1
  107.1 2.4 %draws.1 = (f32[8,16,128]{2,1,0:T(8,128)S(1)}, f32[1,16384]{1,0:T(1,128)S(1)}, f32[1,16384]{1,0:T(1,128)S(1)}, f32[1,16384]{1,0:T(1,128)S(1)}) custom-call(s32[128]{0:T(128)S(1)} %copy-done.2, f32[8,128]{1,0:T(8,128)S(1)} %last.1.message.m0, f32[8,128]{1,0:T(8,128)S(1)} %collective-permute-done.3.m1, f32[8,128]{1,0:T(8,128)S(1)} %collective-permute-done.4.m2, ...), custom_call_target="tpu_custom_call" | custom-call | tf_op jit(solution)/shard_map/draws/pallas_call | solution.py:483
  109.6 8.5 %all_to_all.45.arrived = f32[8,16,128]{2,1,0:T(8,128)S(1)} all-to-all(f32[8,16,128]{2,1,0:T(8,128)S(1)} %get-tuple-element.34), channel_id=1, replica_groups=mesh['y'=4,'z'=8,'core'=2,'cell'=4] {'y','core'}, dimensions={0} | all-to-all | bytes 131072 | tf_op jit(solution)/shard_map/all_to_all | solution.py:397
  118.1 9.7 %all_to_all.46.arrived = f32[8,16,128]{2,1,0:T(8,128)S(1)} all-to-all(f32[8,16,128]{2,1,0:T(8,128)S(1)} %relay.7), channel_id=1, replica_groups=mesh['y'=4,'z'=8,'core'=2,'cell'=4] {'z'}, dimensions={0} | all-to-all | bytes 131072 | tf_op jit(solution)/shard_map/all_to_all | solution.py:403
  127.8 0.8 finish.1
  (9 shorter events, 0.1 us)
Async XLA Ops:
  0.6 33.4 %copy-start.1 = (s32[1,2]{1,0:T(1,128)S(1)}, s32[1,2]{1,0:T(1,128)}, u32[]{:S(2)}) copy-start(s32[1,2]{1,0:T(1,128)} %cells.7) | copy-start | bytes 28
  0.6 33.3 %copy-start.2 = (s32[128]{0:T(128)S(1)}, s32[128]{0:T(128)}, u32[]{:S(2)}) copy-start(s32[128]{0:T(128)} %cohorts.7) | copy-start | bytes 1540
  0.6 33.3 %copy-start = (f32[8,16384]{1,0:T(8,128)S(1)}, f32[8,16384]{1,0:T(8,128)}, u32[]{:S(2)}) copy-start(f32[8,16384]{1,0:T(8,128)} %y_hbm.3) | copy-start | bytes 1572868
  31.5 4.5 %collective-permute-start = (f32[8,2,2176]{2,1,0:T(2,128)S(1)}, f32[8,2,2176]{2,1,0:T(2,128)S(1)}, u32[]{:S(2)}, u32[]{:S(2)}) collective-permute-start(f32[8,2,2176]{2,1,0:T(2,128)S(1)} %all_to_all.41.own), channel_id=1, source_target_pairs={{0,4},{4,0},{1,5},{5,1},{2,6},{6,2},{3,7},{7,3},{8,12},{12,8},{9,1... | collective-permute-start | bytes 417800 | tf_op jit(solution)/shard_map/ppermute | solution.py:393
  61.9 3.6 %collective-permute-start.1 = (f32[8,2,2816]{2,1,0:T(2,128)S(1)}, f32[8,2,2816]{2,1,0:T(2,128)S(1)}, u32[]{:S(2)}, u32[]{:S(2)}) collective-permute-start(f32[8,2,2816]{2,1,0:T(2,128)S(1)} %all_to_all.43.own), channel_id=1, source_target_pairs={{0,4},{4,0},{1,5},{5,1},{2,6},{6,2},{3,7},{7,3},{8,12},{12,8},{9,1... | collective-permute-start | bytes 540680 | tf_op jit(solution)/shard_map/ppermute | solution.py:393
  81.6 11.1 %all-to-all-start.5 = ((f32[8,2,2176]{2,1,0:T(2,128)}), f32[8,2,2176]{2,1,0:T(2,128)S(1)}, u32[]{:S(2)}, u32[]{:S(2)}) async-start(f32[8,2,2176]{2,1,0:T(2,128)} %relay.6), calls=%async_computation.5 | async-start | bytes 278528 | tf_op jit(solution)/shard_map/all_to_all | solution.py:403
  92.7 3.4 %collective-permute-start.2 = (f32[8,2,2176]{2,1,0:T(2,128)S(1)}, f32[8,2,2176]{2,1,0:T(2,128)S(1)}, u32[]{:S(2)}, u32[]{:S(2)}) collective-permute-start(f32[8,2,2176]{2,1,0:T(2,128)S(1)} %all-to-all-done.5.own), channel_id=1, source_target_pairs={{0,4},{4,0},{1,5},{5,1},{2,6},{6,2},{3,7},{7,3},{8,12},{12,8},{9,1... | collective-permute-start | bytes 417800 | tf_op jit(solution)/shard_map/ppermute | solution.py:393
  100.1 7.0 %collective-permute-start.5 = (f32[8,128]{1,0:T(8,128)S(1)}, f32[8,128]{1,0:T(8,128)S(1)}, u32[]{:S(2)}, u32[]{:S(2)}) collective-permute-start(f32[8,128]{1,0:T(8,128)S(1)} %last.1.message.m0), channel_id=1, source_target_pairs={{0,3},{1,2},{2,1},{3,0},{4,7},{5,6},{6,5},{7,4},{8,11},{9,10},{10,... | collective-permute-start | bytes 12296 | tf_op jit(solution)/shard_map/ppermute | solution.py:481
  102.7 4.5 %collective-permute-start.4 = (f32[8,128]{1,0:T(8,128)S(1)}, f32[8,128]{1,0:T(8,128)S(1)}, u32[]{:S(2)}, u32[]{:S(2)}) collective-permute-start(f32[8,128]{1,0:T(8,128)S(1)} %last.1.message.m0), channel_id=1, source_target_pairs={{0,2},{1,3},{2,0},{3,1},{4,6},{5,7},{6,4},{7,5},{8,10},{9,11},{10,... | collective-permute-start | bytes 12296 | tf_op jit(solution)/shard_map/ppermute | solution.py:481
  103.2 4.0 %collective-permute-start.3 = (f32[8,128]{1,0:T(8,128)S(1)}, f32[8,128]{1,0:T(8,128)S(1)}, u32[]{:S(2)}, u32[]{:S(2)}) collective-permute-start(f32[8,128]{1,0:T(8,128)S(1)} %last.1.message.m0), channel_id=1, source_target_pairs={{0,1},{1,0},{2,3},{3,2},{4,5},{5,4},{6,7},{7,6},{8,9},{9,8},{10,11... | collective-permute-start | bytes 12296 | tf_op jit(solution)/shard_map/ppermute | solution.py:481

commit v4 on v3

--- a/solution.py
+++ b/solution.py
@@ -206,8 +206,7 @@
     write_payload(out, folded, (total[WIDTH : WIDTH + 1], jnp.where(first_lane, scalar, diagonal)))
 
 
-def control_kernel(cells, cohorts, x, xt, y, out):
-    group, period = cells[0, 0], cells[0, 1]
+def control_rows(group, period, cohorts, x, xt, y):
     per = CHUNK // WIDTH
     total = jnp.zeros((WIDTH + 16, WIDTH), F32)
     for i in range(x.shape[0] // CHUNK):
@@ -222,17 +221,16 @@
         left = jnp.concatenate(left, axis=1)
         total = total + jnp.dot(left, x[chunk_of(i), :], preferred_element_type=F32)
     folded, diagonal = fold(total[:WIDTH])
-    out[0:64, :] = folded
-    out[64:72, :] = jnp.concatenate(
-        [total[WIDTH : WIDTH + 1], diagonal, jnp.zeros((6, WIDTH), F32)], axis=0
-    )
+    return folded, jnp.concatenate([total[WIDTH : WIDTH + 1], diagonal], axis=0)
 
 
 def newton_kernel(
-    first, cells, cohorts, own, other, x, xt, before, control, coefs, keep, out
+    first, cells, cohorts, own, other, x, xt, before, y, coefs, keep, out
 ):
     group, period = cells[0, 0], cells[0, 1]
     per = CHUNK // WIDTH
+    if first:
+        control, ends = control_rows(group, period, cohorts, x, xt, y)
     mine = summed(own)
     core = lax.axis_index("core")
     folded, row, diagonal = halves(core, unpacked(mine, 0, 33), unpacked(summed(other), 0, 33))
@@ -266,7 +264,7 @@
     folded, diagonal = fold(total[:WIDTH])
     if first:
         more = [
-            jnp.concatenate([control[64:66, :], control[8 * p : 8 * p + 8, :]], axis=0)
+            jnp.concatenate([ends, control[8 * p : 8 * p + 8]], axis=0)
             for p in range(out.shape[0])
         ]
     else:
@@ -445,9 +443,6 @@
     )(*(pltpu.with_memory_space_constraint(v, pltpu.HBM) for v in (cells, cohorts, covariates, outcomes)))
     halfway = to_pairs(payload)
     arrived = to_line(halfway, 17 * WIDTH)
-    control = call(
-        control_kernel, "control", [shape(72, WIDTH)], [SMEM, SMEM, FREE, FREE, FREE], cost=cost
-    )(cells, cohorts, tall, wide, outcomes)[0]
     coefs = jnp.zeros((8, WIDTH), F32)
     kept = []
     for step in range(2):
@@ -455,8 +450,8 @@
             functools.partial(newton_kernel, step == 0),
             "newton",
             [eight, eight, shape(pairs, 2, 22 * WIDTH)],
-            [SMEM, SMEM, VMEM, VMEM, FREE, FREE, VMEM, VMEM],
-        )(cells, cohorts, arrived, swap_cores(arrived), tall, wide, coefs, control)
+            [SMEM, SMEM, VMEM, VMEM, FREE, FREE, VMEM, FREE],
+        )(cells, cohorts, arrived, swap_cores(arrived), tall, wide, coefs, outcomes)
         kept.append(keep)
         halfway = to_pairs(payload)
         arrived = to_line(halfway, (22 - 5 * step) * WIDTH)

time: 129 us -> 129 us (level)
  Pallas kernels: 34.7 us -> 33.3 us
    pallas_call x1 -> x0, Pallas kernels: 1.99 us -> none  [shards(): call(control_kernel, 'control', [shape(72, WIDTH)], [SMEM, SMEM, FREE, FR...]
  transfers between devices with their start and end apart: 7 -> 7, of which waited for: 3 -> 4; matrix products, arithmetic and copies ran while one was open for 0% -> 0% of each run, Pallas kernels for 7% -> 6%
where the time goes in v4:
time: 129 us
  blocking collectives  73 us (57%)
  Pallas kernels  33.3 us (26%)
  starting transfers between devices  14.2 us (11%)
  waiting for transfers between devices  7.35 us (6%)
    all_to_all x4, blocking collectives, to_pairs(): return lax.all_to_all(payload, ('y', 'core'), 0, 0)  36.6 us
    all_to_all x3, blocking collectives, to_line(): return lax.all_to_all(copies[0], 'z', 0, 0)  36.4 us
    pallas_call x2, Pallas kernels, shards(): call(functools.partial(newton_kernel, step == 0), 'newton', [eight, eight...  14.3 us
    ppermute x3, starting transfers between devices, swap_cores(): return lax.ppermute(value, 'core', [(0, 1), (1, 0)])  7.45 us
    all_to_all x1, waiting for transfers between devices, to_line(): return lax.all_to_all(copies[0], 'z', 0, 0)  4.3 us
    pallas_call x1, Pallas kernels, shards(): call(last_kernel, 'last', [eight], [SMEM] + [VMEM] * 5)  4.03 us
    pallas_call x1, Pallas kernels, shards(): call(first_kernel, 'first', [shape(rows_here, WIDTH, dtype=BF16), shape(W...  3.86 us
    pallas_call x1, Pallas kernels, shards(): call(bring_kernel, 'bring', [shape(rows_here, WIDTH, dtype=BF16), shape(*...  3.66 us
  transfers between devices with their start and end apart: 7, of which 4 were waited for; matrix products, arithmetic and copies ran while one was open for 0% of the time, Pallas kernels for 6%

profile of v4, /device:TPU:1, one launch (start us, length us, event | category | flops | bytes accessed | tf_op | source)
XLA Modules:
  0.0 128.5 jit_solution(8383355074061804048)
XLA Ops:
  0.6 0.0 copy-start
  0.7 3.9 %first.1 = (bf16[16384,128]{1,0:T(8,128)(2,1)S(1)}, bf16[128,16384]{1,0:T(8,128)(2,1)S(1)}, f32[8,2,2176]{2,1,0:T(2,128)S(1)}) custom-call(s32[1,2]{1,0:T(1,128)} %cells.5, s32[128]{0:T(128)} %cohorts.5, bf16[16384,128]{1,0:T(8,128)(2,1)} %x_hbm.3, f32[8,16384]{1,0:T(8,128)} %y_hbm.3), custom_call_target="tpu_custom_call" | custom-call | tf_op jit(solution)/shard_map/first/pallas_call | solution.py:425
  4.5 11.1 %all_to_all.40.arrived = f32[8,2,2176]{2,1,0:T(2,128)S(1)} all-to-all(f32[8,2,2176]{2,1,0:T(2,128)S(1)} %get-tuple-element.20), channel_id=1, replica_groups=mesh['y'=4,'z'=8,'core'=2,'cell'=4] {'y','core'}, dimensions={0} | all-to-all | bytes 278528 | tf_op jit(solution)/shard_map/all_to_all | solution.py:395
  15.7 15.8 %all_to_all.41.own = f32[8,2,2176]{2,1,0:T(2,128)S(1)} all-to-all(f32[8,2,2176]{2,1,0:T(2,128)S(1)} %relay.4), channel_id=1, replica_groups=mesh['y'=4,'z'=8,'core'=2,'cell'=4] {'z'}, dimensions={0} | all-to-all | bytes 278528 | tf_op jit(solution)/shard_map/all_to_all | solution.py:401
  31.5 2.5 %collective-permute-start = (f32[8,2,2176]{2,1,0:T(2,128)S(1)}, f32[8,2,2176]{2,1,0:T(2,128)S(1)}, u32[]{:S(2)}, u32[]{:S(2)}) collective-permute-start(f32[8,2,2176]{2,1,0:T(2,128)S(1)} %all_to_all.41.own), channel_id=1, source_target_pairs={{0,4},{4,0},{1,5},{5,1},{2,6},{6,2},{3,7},{7,3},{8,12},{12,8},{9,1... | collective-permute-start | bytes 417800 | tf_op jit(solution)/shard_map/ppermute | solution.py:391
  34.0 1.0 collective-permute-done.other
  35.0 0.0 copy-done.1
  35.0 7.4 %newton.2 = (f32[8,128]{1,0:T(8,128)S(1)}, f32[8,128]{1,0:T(8,128)S(1)}, f32[8,2,2816]{2,1,0:T(2,128)S(1)}) custom-call(s32[1,2]{1,0:T(1,128)S(1)} %copy-done.1, s32[128]{0:T(128)S(1)} %copy-done.2, f32[8,2,2176]{2,1,0:T(2,128)S(1)} %all_to_all.41.own, f32[8,2,2176]{2,1,0:T(2,128)S(1)} %collective-permute-done.other, ...), custom_call_target="tpu_custom_call" | custom-call | tf_op jit(solution)/shard_map/newton/pallas_call | solution.py:449
  42.4 8.5 %all_to_all.42.arrived = f32[8,2,2816]{2,1,0:T(2,128)S(1)} all-to-all(f32[8,2,2816]{2,1,0:T(2,128)S(1)} %get-tuple-element.23), channel_id=1, replica_groups=mesh['y'=4,'z'=8,'core'=2,'cell'=4] {'y','core'}, dimensions={0} | all-to-all | bytes 360448 | tf_op jit(solution)/shard_map/all_to_all | solution.py:395
  50.9 10.9 %all_to_all.43.own = f32[8,2,2816]{2,1,0:T(2,128)S(1)} all-to-all(f32[8,2,2816]{2,1,0:T(2,128)S(1)} %relay.5), channel_id=1, replica_groups=mesh['y'=4,'z'=8,'core'=2,'cell'=4] {'z'}, dimensions={0} | all-to-all | bytes 360448 | tf_op jit(solution)/shard_map/all_to_all | solution.py:401
  61.8 2.6 %collective-permute-start.1 = (f32[8,2,2816]{2,1,0:T(2,128)S(1)}, f32[8,2,2816]{2,1,0:T(2,128)S(1)}, u32[]{:S(2)}, u32[]{:S(2)}) collective-permute-start(f32[8,2,2816]{2,1,0:T(2,128)S(1)} %all_to_all.43.own), channel_id=1, source_target_pairs={{0,4},{4,0},{1,5},{5,1},{2,6},{6,2},{3,7},{7,3},{8,12},{12,8},{9,1... | collective-permute-start | bytes 540680 | tf_op jit(solution)/shard_map/ppermute | solution.py:391
  64.3 1.0 collective-permute-done.1.other
  65.4 6.9 %newton.3 = (f32[8,128]{1,0:T(8,128)S(1)}, f32[8,128]{1,0:T(8,128)S(1)}, f32[8,2,2816]{2,1,0:T(2,128)S(1)}) custom-call(s32[1,2]{1,0:T(1,128)S(1)} %copy-done.1, s32[128]{0:T(128)S(1)} %copy-done.2, f32[8,2,2816]{2,1,0:T(2,128)S(1)} %all_to_all.43.own, f32[8,2,2816]{2,1,0:T(2,128)S(1)} %collective-permute-done.1.other, ...), custom_call_target="tpu_custom_call" | custom-call | tf_op jit(solution)/shard_map/newton/pallas_call | solution.py:449
  72.3 8.5 %all_to_all.44.arrived = f32[8,2,2816]{2,1,0:T(2,128)S(1)} all-to-all(f32[8,2,2816]{2,1,0:T(2,128)S(1)} %get-tuple-element.25), channel_id=1, replica_groups=mesh['y'=4,'z'=8,'core'=2,'cell'=4] {'y','core'}, dimensions={0} | all-to-all | bytes 360448 | tf_op jit(solution)/shard_map/all_to_all | solution.py:395
  80.8 0.7 relay.6
  81.5 3.4 %all-to-all-start.5 = ((f32[8,2,2176]{2,1,0:T(2,128)}), f32[8,2,2176]{2,1,0:T(2,128)S(1)}, u32[]{:S(2)}, u32[]{:S(2)}) async-start(f32[8,2,2176]{2,1,0:T(2,128)} %relay.6), calls=%async_computation.5 | async-start | bytes 278528 | tf_op jit(solution)/shard_map/all_to_all | solution.py:401
  84.8 3.4 %ols.1.control = f32[8,128]{1,0:T(8,128)S(1)} custom-call(f32[8,2,2816]{2,1,0:T(2,128)S(1)} %all_to_all.44.arrived, f32[8,128]{1,0:T(8,128)S(1)} %get-tuple-element.26.extras), custom_call_target="tpu_custom_call" | custom-call | flops 8589934592 | bytes 10485760 | tf_op jit(solution)/shard_map/ols/pallas_call | solution.py:458
  88.3 4.3 %all-to-all-done.5.own = f32[8,2,2176]{2,1,0:T(2,128)S(1)} async-done(((f32[8,2,2176]{2,1,0:T(2,128)}), f32[8,2,2176]{2,1,0:T(2,128)S(1)}, u32[]{:S(2)}, u32[]{:S(2)}) %all-to-all-start.5) | async-done | bytes 139296 | tf_op jit(solution)/shard_map/all_to_all | solution.py:401
  92.6 2.4 %collective-permute-start.2 = (f32[8,2,2176]{2,1,0:T(2,128)S(1)}, f32[8,2,2176]{2,1,0:T(2,128)S(1)}, u32[]{:S(2)}, u32[]{:S(2)}) collective-permute-start(f32[8,2,2176]{2,1,0:T(2,128)S(1)} %all-to-all-done.5.own), channel_id=1, source_target_pairs={{0,4},{4,0},{1,5},{5,1},{2,6},{6,2},{3,7},{7,3},{8,12},{12,8},{9,1... | collective-permute-start | bytes 417800 | tf_op jit(solution)/shard_map/ppermute | solution.py:391
  95.0 1.0 collective-permute-done.2.other
  96.0 4.0 %last.1.message.m0 = f32[8,128]{1,0:T(8,128)S(1)} custom-call(s32[1,2]{1,0:T(1,128)S(1)} %copy-done.1, f32[8,2,2176]{2,1,0:T(2,128)S(1)} %all-to-all-done.5.own, f32[8,2,2176]{2,1,0:T(2,128)S(1)} %collective-permute-done.2.other, f32[8,128]{1,0:T(8,128)S(1)} %ols.1.control, f32[8,128]{1,0:T(8,128)S(1)} %get-tuple-element.29.before, ...), custom_call_target="tpu_custom_call" | custom-call | tf_op jit(solution)/shard_map/last/pallas_call | solution.py:460
  100.0 2.6 %collective-permute-start.5 = (f32[8,128]{1,0:T(8,128)S(1)}, f32[8,128]{1,0:T(8,128)S(1)}, u32[]{:S(2)}, u32[]{:S(2)}) collective-permute-start(f32[8,128]{1,0:T(8,128)S(1)} %last.1.message.m0), channel_id=1, source_target_pairs={{0,3},{1,2},{2,1},{3,0},{4,7},{5,6},{6,5},{7,4},{8,11},{9,10},{10,... | collective-permute-start | bytes 12296 | tf_op jit(solution)/shard_map/ppermute | solution.py:476
  102.6 0.5 collective-permute-start.4
  103.1 0.3 collective-permute-start.3
  103.3 3.7 %bring.1 = (bf16[16384,128]{1,0:T(8,128)(2,1)S(1)}, f32[8,16384]{1,0:T(8,128)S(1)}, bf16[16384,128]{1,0:T(8,128)(2,1)S(1)}) custom-call(f32[8,128]{1,0:T(8,128)S(1)} %last.1.message.m0, bf16[16384,128]{1,0:T(8,128)(2,1)} %x_hbm.3, f32[8,16384]{1,0:T(8,128)} %y_hbm.3, bf16[16384,128]{1,0:T(8,128)(2,1)} %mult_hbm.1), custom_call_target="tpu_custom_call" | custom-call | flops 8589934592 | bytes 10485760 | tf_op jit(solution)/shard_map/bring/pallas_call | solution.py:463
  107.0 0.0 collective-permute-done.5.m3
  107.0 0.0 collective-permute-done.4.m2
  107.0 0.0 collective-permute-done.3.m1
  107.0 2.4 %draws.1 = (f32[8,16,128]{2,1,0:T(8,128)S(1)}, f32[1,16384]{1,0:T(1,128)S(1)}, f32[1,16384]{1,0:T(1,128)S(1)}, f32[1,16384]{1,0:T(1,128)S(1)}) custom-call(s32[128]{0:T(128)S(1)} %copy-done.2, f32[8,128]{1,0:T(8,128)S(1)} %last.1.message.m0, f32[8,128]{1,0:T(8,128)S(1)} %collective-permute-done.3.m1, f32[8,128]{1,0:T(8,128)S(1)} %collective-permute-done.4.m2, ...), custom_call_target="tpu_custom_call" | custom-call | tf_op jit(solution)/shard_map/draws/pallas_call | solution.py:478
  109.5 8.5 %all_to_all.45.arrived = f32[8,16,128]{2,1,0:T(8,128)S(1)} all-to-all(f32[8,16,128]{2,1,0:T(8,128)S(1)} %get-tuple-element.34), channel_id=1, replica_groups=mesh['y'=4,'z'=8,'core'=2,'cell'=4] {'y','core'}, dimensions={0} | all-to-all | bytes 131072 | tf_op jit(solution)/shard_map/all_to_all | solution.py:395
  118.0 9.7 %all_to_all.46.arrived = f32[8,16,128]{2,1,0:T(8,128)S(1)} all-to-all(f32[8,16,128]{2,1,0:T(8,128)S(1)} %relay.7), channel_id=1, replica_groups=mesh['y'=4,'z'=8,'core'=2,'cell'=4] {'z'}, dimensions={0} | all-to-all | bytes 131072 | tf_op jit(solution)/shard_map/all_to_all | solution.py:401
  127.7 0.8 finish.1
  (8 shorter events, 0.1 us)
Async XLA Ops:
  0.6 34.3 %copy-start.1 = (s32[1,2]{1,0:T(1,128)S(1)}, s32[1,2]{1,0:T(1,128)}, u32[]{:S(2)}) copy-start(s32[1,2]{1,0:T(1,128)} %cells.5) | copy-start | bytes 28
  0.6 34.3 %copy-start.2 = (s32[128]{0:T(128)S(1)}, s32[128]{0:T(128)}, u32[]{:S(2)}) copy-start(s32[128]{0:T(128)} %cohorts.5) | copy-start | bytes 1540
  0.6 34.3 %copy-start = (f32[8,16384]{1,0:T(8,128)S(1)}, f32[8,16384]{1,0:T(8,128)}, u32[]{:S(2)}) copy-start(f32[8,16384]{1,0:T(8,128)} %y_hbm.3) | copy-start | bytes 1572868
  31.5 3.5 %collective-permute-start = (f32[8,2,2176]{2,1,0:T(2,128)S(1)}, f32[8,2,2176]{2,1,0:T(2,128)S(1)}, u32[]{:S(2)}, u32[]{:S(2)}) collective-permute-start(f32[8,2,2176]{2,1,0:T(2,128)S(1)} %all_to_all.41.own), channel_id=1, source_target_pairs={{0,4},{4,0},{1,5},{5,1},{2,6},{6,2},{3,7},{7,3},{8,12},{12,8},{9,1... | collective-permute-start | bytes 417800 | tf_op jit(solution)/shard_map/ppermute | solution.py:391
  61.8 3.6 %collective-permute-start.1 = (f32[8,2,2816]{2,1,0:T(2,128)S(1)}, f32[8,2,2816]{2,1,0:T(2,128)S(1)}, u32[]{:S(2)}, u32[]{:S(2)}) collective-permute-start(f32[8,2,2816]{2,1,0:T(2,128)S(1)} %all_to_all.43.own), channel_id=1, source_target_pairs={{0,4},{4,0},{1,5},{5,1},{2,6},{6,2},{3,7},{7,3},{8,12},{12,8},{9,1... | collective-permute-start | bytes 540680 | tf_op jit(solution)/shard_map/ppermute | solution.py:391
  81.5 11.1 %all-to-all-start.5 = ((f32[8,2,2176]{2,1,0:T(2,128)}), f32[8,2,2176]{2,1,0:T(2,128)S(1)}, u32[]{:S(2)}, u32[]{:S(2)}) async-start(f32[8,2,2176]{2,1,0:T(2,128)} %relay.6), calls=%async_computation.5 | async-start | bytes 278528 | tf_op jit(solution)/shard_map/all_to_all | solution.py:401
  92.6 3.4 %collective-permute-start.2 = (f32[8,2,2176]{2,1,0:T(2,128)S(1)}, f32[8,2,2176]{2,1,0:T(2,128)S(1)}, u32[]{:S(2)}, u32[]{:S(2)}) collective-permute-start(f32[8,2,2176]{2,1,0:T(2,128)S(1)} %all-to-all-done.5.own), channel_id=1, source_target_pairs={{0,4},{4,0},{1,5},{5,1},{2,6},{6,2},{3,7},{7,3},{8,12},{12,8},{9,1... | collective-permute-start | bytes 417800 | tf_op jit(solution)/shard_map/ppermute | solution.py:391
  100.0 7.0 %collective-permute-start.5 = (f32[8,128]{1,0:T(8,128)S(1)}, f32[8,128]{1,0:T(8,128)S(1)}, u32[]{:S(2)}, u32[]{:S(2)}) collective-permute-start(f32[8,128]{1,0:T(8,128)S(1)} %last.1.message.m0), channel_id=1, source_target_pairs={{0,3},{1,2},{2,1},{3,0},{4,7},{5,6},{6,5},{7,4},{8,11},{9,10},{10,... | collective-permute-start | bytes 12296 | tf_op jit(solution)/shard_map/ppermute | solution.py:476
  102.6 4.5 %collective-permute-start.4 = (f32[8,128]{1,0:T(8,128)S(1)}, f32[8,128]{1,0:T(8,128)S(1)}, u32[]{:S(2)}, u32[]{:S(2)}) collective-permute-start(f32[8,128]{1,0:T(8,128)S(1)} %last.1.message.m0), channel_id=1, source_target_pairs={{0,2},{1,3},{2,0},{3,1},{4,6},{5,7},{6,4},{7,5},{8,10},{9,11},{10,... | collective-permute-start | bytes 12296 | tf_op jit(solution)/shard_map/ppermute | solution.py:476
  103.1 3.9 %collective-permute-start.3 = (f32[8,128]{1,0:T(8,128)S(1)}, f32[8,128]{1,0:T(8,128)S(1)}, u32[]{:S(2)}, u32[]{:S(2)}) collective-permute-start(f32[8,128]{1,0:T(8,128)S(1)} %last.1.message.m0), channel_id=1, source_target_pairs={{0,1},{1,0},{2,3},{3,2},{4,5},{5,4},{6,7},{7,6},{8,9},{9,8},{10,11... | collective-permute-start | bytes 12296 | tf_op jit(solution)/shard_map/ppermute | solution.py:476
